TPU v7x, 32 devices: a whole 2x2x4 slice. The times are simulated.
32 devices in a mesh: groups: 2 (over y), tensor: 4 (over z), dp: 2 (over x), section: 2 (over core).
Axes of the slice: x: 2, y: 2, z: 4, core: 2. Of those that a mesh axis runs over, the one named last changes fastest.
Arguments:
- attended: bfloat16 [4, 4096, 4096], P(('groups', 'dp'), 'tensor', 'section'), parts along dimension 0, may hold values from -6 to 6
- weight_tiles: bfloat16 [4, 2, 256, 128, 128], P('tensor', 'section'), may hold values from -0.125 to 0.125
- block_lists: int32 [4, 2, 256], P('tensor', 'section'), may hold values from 0 to 255, as said below
- kept_counts: int32 [4, 2], P('tensor', 'section'), may hold values from 64 to 256, as said below
- out_grad: bfloat16 [4, 4096, 8192], P(('groups', 'dp'), None, ('tensor', 'section')), parts along dimension 0, may hold values from -6 to 6
Outputs:
- projected: bfloat16 [4, 4096, 8192], P(('groups', 'dp'), None, 'tensor'), parts along dimension 0
- tiles_grad: float32 [8, 2, 256, 128, 128], P(('groups', 'tensor'), 'section', 'dp'), parts along dimension 0
There are 2 independent parts, one for each index of `groups`. A program takes and returns all parts, laid end to end along the dimension named above; an argument that names none is the same for every part. Nothing has to cross between parts.
Inputs may be any that keep to these rules, and one draw needn't show every extreme that they name: `kept_counts`: every shard keeps at least a quarter of its 256 blocks; some shard keeps all of them; on average about half are kept. `block_lists`: each shard's list names each of its 256 local blocks once; the first kept_counts entries are its kept blocks in increasing order, the rest its other blocks in increasing order.
All inputs are finite; a program needn't handle non-finite values.
Results may differ from a plain program's by a relative error of at most 0.009.
Values may be sent and summed in bfloat16 or wider, within the bound.
A program may use at most 192 MiB of HBM per device.

v0:
```python
import jax
import jax.numpy as jnp
from jax import lax
from jax.sharding import PartitionSpec as P


def local(attended, weight_tiles, block_lists, kept_counts, out_grad):
    tile_width = weight_tiles.shape[-1]
    slot_count = weight_tiles.shape[2]
    in_width = attended.shape[2]
    row_blocks = in_width // tile_width
    col_blocks = slot_count // row_blocks
    live_flag = jnp.arange(slot_count) < kept_counts[0, 0]
    tile_set = jnp.where(
        live_flag[:, None, None], weight_tiles[0, 0], jnp.zeros_like(weight_tiles[0, 0])
    )
    slot_block = block_lists[0, 0]
    place_hot = (slot_block[None, :] == jnp.arange(slot_count)[:, None]).astype(jnp.bfloat16)
    placed = jnp.einsum(
        "pk,kbc->pbc", place_hot, tile_set, preferred_element_type=jnp.float32
    ).astype(jnp.bfloat16)
    placed = placed.reshape(row_blocks, col_blocks, tile_width, tile_width)
    dense = jnp.transpose(placed, (0, 2, 1, 3)).reshape(
        row_blocks * tile_width, col_blocks * tile_width
    )
    columns = lax.all_gather(out_grad, "section", axis=2, tiled=True)
    grad_cols = columns[0]
    gathered = lax.all_gather(attended, "tensor", axis=1, tiled=True)[0]
    partial_out = jnp.dot(gathered, dense, preferred_element_type=jnp.float32)
    dense_grad = jnp.einsum("ti,to->io", gathered, grad_cols, preferred_element_type=jnp.float32)
    projected = lax.psum(partial_out.astype(jnp.bfloat16), "section")[None]
    rounded = dense_grad.astype(jnp.bfloat16)
    blocks = rounded.reshape(row_blocks, tile_width, col_blocks, tile_width)
    blocks = jnp.transpose(blocks, (0, 2, 1, 3)).reshape(slot_count, tile_width, tile_width)
    picked = jnp.einsum("pk,pbc->kbc", place_hot, blocks, preferred_element_type=jnp.float32)
    tile_sum = jnp.where(live_flag[:, None, None], picked, jnp.zeros_like(picked))
    tiles_grad = lax.psum_scatter(
        tile_sum.astype(jnp.bfloat16), "dp", scatter_dimension=0, tiled=True
    ).astype(jnp.float32)
    return (projected, tiles_grad[None, None])


def solution(mesh):
    in_specs = (
        P(("groups", "dp"), "tensor", "section"),
        P("tensor", "section", None, None, None),
        P("tensor", "section", None),
        P("tensor", "section"),
        P(("groups", "dp"), None, ("tensor", "section")),
    )
    out_specs = (
        P(("groups", "dp"), None, "tensor"),
        P(("groups", "tensor"), "section", "dp", None, None),
    )
    return jax.shard_map(local, mesh=mesh, in_specs=in_specs, out_specs=out_specs, check_vma=False)
```

profile of v0, /device:TPU:0, one launch (start us, length us, event | category | flops | bytes accessed | tf_op | source)
XLA Modules:
  0.0 600.7 jit_solution(762937150078674743)
XLA Ops:
  7.2 0.0 all-gather.5.cloned.1.call-start
  7.2 0.7 all-gather.5.cloned.1.call-update
  7.9 0.0 all-gather.3.cloned.1.call-start
  7.9 0.7 all-gather.3.cloned.1.call-update
  8.6 0.0 reduce-scatter.2.cloned.1.call-start
  9.4 33.0 %all-gather.5.cloned.1.call-done = bf16[1,4096,2048]{2,1,0:T(8,128)(2,1)} async-done(((bf16[1,4096,1024]{2,1,0:T(8,128)(2,1)}), bf16[1,4096,2048]{2,1,0:T(8,128)(2,1)}) %all-gather.5.cloned.1.call-update) | async-done | bytes 16777232 | tf_op jit(solution)/shard_map/all_gather | solution.py:26
  42.4 289.5 %all-gather.3.cloned.1.call-done = bf16[1,4096,2048]{2,1,0:T(8,128)(2,1)} async-done(((bf16[1,1024,2048]{2,1,0:T(8,128)(2,1)}), bf16[1,4096,2048]{2,1,0:T(8,128)(2,1)}) %all-gather.3.cloned.1.call-update) | async-done | bytes 16777232 | tf_op jit(solution)/shard_map/all_gather | solution.py:28
  331.9 43.3 %convert_bitcast_fusion.1 = bf16[256,8,16,128]{3,1,2,0:T(8,128)(2,1)} fusion(bf16[1,4096,2048]{2,1,0:T(8,128)(2,1)} %all-gather.5.cloned.1.call-done, bf16[1,4096,2048]{2,1,0:T(8,128)(2,1)} %all-gather.3.cloned.1.call-done), kind=kOutput, calls=%fused_computation.13 | convolution fusion | flops 34363932672 | bytes 41943040 | tf_op jit(solution)/shard_map/ti,to->io/dot_general | solution.py:30
  375.2 9.9 %copy.21 = bf16[256,8,16,128]{3,2,1,0:T(8,128)(2,1)} copy(bf16[256,8,16,128]{3,1,2,0:T(8,128)(2,1)} %convert_bitcast_fusion.1) | data formatting | bytes 16777216
  385.1 8.6 %bitcast_bitcast_fusion = bf16[16,16,128,128]{3,1,2,0:T(8,128)(2,1)} fusion(bf16[16,128,16,128]{3,2,1,0:T(8,128)(2,1)} %bitcast.51), kind=kLoop, calls=%fused_computation.7 | loop fusion | bytes 16777216 | tf_op jit(solution)/shard_map/transpose | solution.py:34
  393.7 0.0 copy-start
  393.7 9.3 %copy.15 = bf16[16,16,128,128]{3,1,0,2:T(8,128)(2,1)} copy(bf16[16,16,128,128]{3,1,2,0:T(8,128)(2,1)} %bitcast_bitcast_fusion) | data formatting | bytes 16777216 | tf_op jit(solution)/shard_map/transpose | solution.py:34
  403.0 0.0 copy-done
  403.0 8.0 %select_convert_fusion = bf16[256,128,128]{2,0,1:T(8,128)(2,1)} fusion(bf16[256,128,128]{2,0,1:T(8,128)(2,1)} %bitcast.53, pred[256]{0:T(512)(128)(4,1)S(1)} %iota_compare_fusion.1, s32[256]{0:T(256)S(1)} %bitcast.55), kind=kOutput, calls=%fused_computation.5 | convolution fusion | flops 2155937792 | bytes 16778496 | tf_op jit(solution)/shard_map/pk,pbc->kbc/dot_general | solution.py:35
  410.9 0.0 reduce-scatter.2.cloned.1.call-update
  411.0 0.3 all-reduce.2.cloned.1.call-start
  411.2 13.1 %fusion.16 = bf16[256,128,128]{2,0,1:T(8,128)(2,1)} fusion(bf16[1,1,256,128,128]{4,3,2,1,0:T(8,128)(2,1)} %param.6, pred[256]{0:T(512)(128)(4,1)S(1)} %iota_compare_fusion.1, s32[256]{0:T(256)S(1)} %bitcast.56), kind=kOutput, calls=%fused_computation.15 | convolution fusion | flops 2155937792 | bytes 16778496 | tf_op jit(solution)/shard_map/pk,kbc->pbc/dot_general | solution.py:19
  424.3 8.9 %copy.14 = bf16[16,16,128,128]{3,1,2,0:T(8,128)(2,1)} copy(bf16[16,16,128,128]{3,1,0,2:T(8,128)(2,1)} %bitcast.54) | data formatting | bytes 16777216 | tf_op jit(solution)/shard_map/reshape | solution.py:22
  433.2 45.4 %convert_bitcast_fusion = bf16[1,4096,2048]{1,2,0:T(8,128)(2,1)} fusion(bf16[1,4096,2048]{2,1,0:T(8,128)(2,1)} %all-gather.3.cloned.1.call-done, bf16[256,8,16,128]{3,2,1,0:T(8,128)(2,1)} %bitcast.52), kind=kOutput, calls=%fused_computation.6 | convolution fusion | flops 34368126976 | bytes 41943040 | tf_op jit(solution)/shard_map/dot_general | solution.py:29
  478.6 0.0 all-reduce.2.cloned.1.call-update
  478.6 29.9 %reduce-scatter.2.cloned.1.call-done = bf16[128,128,128]{2,0,1:T(8,128)(2,1)} async-done(((bf16[256,128,128]{2,0,1:T(8,128)(2,1)}), bf16[128,128,128]{2,0,1:T(8,128)(2,1)}) %reduce-scatter.2.cloned.1.call-update) | async-done | bytes 4194320 | tf_op jit(solution)/shard_map/reduce_scatter | solution.py:37
  508.5 3.2 bitcast_convert_fusion
  511.8 9.6 %copy.17 = f32[1,1,128,128,128]{4,3,2,1,0:T(8,128)} copy(f32[1,1,128,128,128]{4,2,3,1,0:T(8,128)S(1)} %bitcast_convert_fusion) | data formatting | bytes 16777216
  521.3 50.4 %all-reduce.2.cloned.1.call-done = bf16[1,4096,2048]{1,2,0:T(8,128)(2,1)} async-done(((bf16[1,4096,2048]{1,2,0:T(8,128)(2,1)}), bf16[1,4096,2048]{1,2,0:T(8,128)(2,1)}) %all-reduce.2.cloned.1.call-update) | async-done | bytes 16777232 | tf_op jit(solution)/shard_map/psum | solution.py:31
  571.7 22.4 %copy.16 = bf16[1,4096,2048]{2,1,0:T(8,128)(2,1)} copy(bf16[1,4096,2048]{1,2,0:T(8,128)(2,1)} %all-reduce.2.cloned.1.call-done) | data formatting | bytes 33554432
  (1 shorter events, 0.0 us)
Async XLA Ops:
  7.2 35.2 %all-gather.5.cloned.1.call-start = ((), (), s32[]{:S(2)}) async-start(), calls=%async_computation.3 | async-start | bytes 25165824 | tf_op jit(solution)/shard_map/all_gather | solution.py:26
  7.9 324.0 %all-gather.3.cloned.1.call-start = ((), (), s32[]{:S(2)}) async-start(), calls=%async_computation.1 | async-start | bytes 20971520 | tf_op jit(solution)/shard_map/all_gather | solution.py:28
  8.6 499.9 %reduce-scatter.2.cloned.1.call-start = ((), (), s32[]{:S(2)}) async-start(), calls=%async_computation.4 | async-start | bytes 12582912 | tf_op jit(solution)/shard_map/reduce_scatter | solution.py:37
  393.7 9.3 %copy-start = (s32[1,1,256]{2,1,0:T(1,128)S(1)}, s32[1,1,256]{2,1,0:T(1,128)}, u32[]{:S(2)}) copy-start(s32[1,1,256]{2,1,0:T(1,128)} %param.7) | copy-start | bytes 3076
  411.0 160.7 %all-reduce.2.cloned.1.call-start = ((), (), s32[]{:S(2)}) async-start(), calls=%async_computation.2 | async-start | bytes 33554432 | tf_op jit(solution)/shard_map/psum | solution.py:31
Sparse Core Ops, SparseCore 0:
  9.6 32.7 all-gather.4
  43.9 287.9 all-gather.2
  411.1 97.4 reduce-scatter.1
  511.6 60.0 all-reduce.1
where the time goes:
time: 602 us; the launch traced here: 601 us
  waiting for transfers between devices  404 us (67%)
  matrix products  110 us (18%)
  local copies, waits for them, and re-layouts  68.7 us (11%)
  between operations  14.4 us (2%)
    all_gather x1, waiting for transfers between devices, local(): gathered = lax.all_gather(attended, 'tensor', axis=1, tiled=True)[0]  290 us
    psum x1, waiting for transfers between devices, local(): projected = lax.psum(partial_out.astype(jnp.bfloat16), 'section')[None]  50.4 us
    dot_general x1, matrix products, local(): partial_out = jnp.dot(gathered, dense, preferred_element_type=jnp.float32)  45.4 us
    dot_general x1, matrix products, local(): jnp.einsum('ti,to->io', gathered, grad_cols, preferred_element_type=jnp.f...  43.3 us
    unnamed x5, local copies, waits for them, and re-layouts  41.9 us
    all_gather x1, waiting for transfers between devices, local(): columns = lax.all_gather(out_grad, 'section', axis=2, tiled=True)  33 us
    reduce_scatter x1, waiting for transfers between devices, local(): lax.psum_scatter(tile_sum.astype(jnp.bfloat16), 'dp', scatter_dimension=0...  29.9 us
    transpose x2, local copies, waits for them, and re-layouts, local(): jnp.transpose(blocks, (0, 2, 1, 3))  17.8 us
  transfers between devices with their start and end apart: 4, of which 4 were waited for; matrix products, arithmetic and copies ran while one was open for 13% of the time, Pallas kernels for 0%

commit v1 on v0

v1 whole, which is shorter than its diff:
```python
import functools

import jax
import jax.numpy as jnp
from jax import lax
from jax.experimental import pallas as pl
from jax.experimental.pallas import tpu as pltpu
from jax.sharding import PartitionSpec as P

WEIGHTS = (6, 5, 3, 2)


def place_kernel(count, slot_ref, live_ref, *refs):
    tiles, out = refs[:count], refs[count]
    width = tiles[0].shape[-1]
    step = pl.program_id(0)
    for u in range(count):
        live = live_ref[step * count + u] > 0
        columns = slice(u * width, (u + 1) * width)

        @pl.when(live)
        def _():
            out[:, columns] = tiles[u][0]

        @pl.when(jnp.logical_not(live))
        def _():
            out[:, columns] = jnp.zeros_like(tiles[u][0])


def place_tiles(tiles, slot_of, live_of, row_blocks, col_blocks):
    width = tiles.shape[-1]
    count = min(8, col_blocks)
    groups = col_blocks // count

    def tile_map(u, i, slot_ref, live_ref):
        return (slot_ref[i * count + u], 0, 0)

    return pl.pallas_call(
        functools.partial(place_kernel, count),
        grid_spec=pltpu.PrefetchScalarGridSpec(
            num_scalar_prefetch=2,
            grid=(row_blocks * groups,),
            in_specs=[
                pl.BlockSpec((1, width, width), functools.partial(tile_map, u))
                for u in range(count)
            ],
            out_specs=pl.BlockSpec(
                (width, width * count), lambda i, s, l: (i // groups, i % groups)
            ),
        ),
        out_shape=jax.ShapeDtypeStruct(
            (row_blocks * width, col_blocks * width), tiles.dtype
        ),
        cost_estimate=pl.CostEstimate(
            flops=0, bytes_accessed=4 * tiles.size, transcendentals=0
        ),
        name="place",
    )(slot_of, live_of, *([tiles] * count))


def pick_kernel(count, block_ref, live_ref, *refs):
    blocks, out = refs[:count], refs[count]
    step = pl.program_id(0)
    for u in range(count):
        live = live_ref[step * count + u] > 0

        @pl.when(live)
        def _():
            out[u] = blocks[u][...]

        @pl.when(jnp.logical_not(live))
        def _():
            out[u] = jnp.zeros_like(blocks[u][...])


def pick_blocks(dense, block_of, live_of, width):
    slots = block_of.shape[0]
    col_blocks = dense.shape[1] // width
    count = 8 if slots % 8 == 0 else 1

    def block_map(u, i, block_ref, live_ref):
        block = block_ref[i * count + u]
        return (block // col_blocks, block % col_blocks)

    return pl.pallas_call(
        functools.partial(pick_kernel, count),
        grid_spec=pltpu.PrefetchScalarGridSpec(
            num_scalar_prefetch=2,
            grid=(slots // count,),
            in_specs=[
                pl.BlockSpec((width, width), functools.partial(block_map, u))
                for u in range(count)
            ],
            out_specs=pl.BlockSpec((count, width, width), lambda i, b, l: (i, 0, 0)),
        ),
        out_shape=jax.ShapeDtypeStruct((slots, width, width), dense.dtype),
        cost_estimate=pl.CostEstimate(
            flops=0, bytes_accessed=8 * slots * width * width, transcendentals=0
        ),
        name="pick",
    )(block_of, live_of, *([dense] * count))


def project_kernel(first, rows_ref, weight_ref, *refs):
    out = refs[-1]
    term = jnp.dot(rows_ref[...], weight_ref[...], preferred_element_type=jnp.float32)
    if not first:
        term = term + refs[0][...]
    out[...] = term.astype(out.dtype)


def project(rows, weight, partial, dtype, begin, height):
    depth, width = weight.shape
    block = min(512, height)
    offset = begin // block
    specs = [
        pl.BlockSpec((block, depth), lambda i: (offset + i, 0)),
        pl.BlockSpec((depth, width), lambda i: (0, 0)),
    ]
    args = [rows, weight]
    if partial is not None:
        specs.append(pl.BlockSpec((block, width), lambda i: (offset + i, 0)))
        args.append(partial)
    moved = (height * depth + depth * width) * 2 + height * width * 8
    return pl.pallas_call(
        functools.partial(project_kernel, partial is None),
        grid=(height // block,),
        in_specs=specs,
        out_specs=pl.BlockSpec((block, width), lambda i: (i, 0)),
        out_shape=jax.ShapeDtypeStruct((height, width), dtype),
        cost_estimate=pl.CostEstimate(
            flops=2 * height * depth * width, bytes_accessed=moved, transcendentals=0
        ),
        input_output_aliases=(
            {2: 0} if partial is not None and partial.dtype == dtype else {}
        ),
        compiler_params=pltpu.CompilerParams(vmem_limit_bytes=40 * 1024 * 1024),
        name="project",
    )(*args)


def combine_kernel(count, *refs):
    total = refs[0][...].astype(jnp.float32)
    for part in refs[1:count]:
        total = total + part[...].astype(jnp.float32)
    refs[-1][...] = total.astype(refs[-1].dtype)


def combine(parts, target, begin, length):
    height, width = parts[0].shape
    block = min(256, height)
    offset = begin // block
    specs = [pl.BlockSpec((block, width), lambda i: (i, 0))] * len(parts)
    args = list(parts)
    if target is not None:
        specs.append(pl.BlockSpec(memory_space=pl.ANY))
        args.append(target)
    return pl.pallas_call(
        functools.partial(combine_kernel, len(parts)),
        grid=(height // block,),
        in_specs=specs,
        out_specs=pl.BlockSpec((block, width), lambda i: (offset + i, 0)),
        out_shape=jax.ShapeDtypeStruct((length, width), parts[0].dtype),
        cost_estimate=pl.CostEstimate(
            flops=0, bytes_accessed=6 * height * width, transcendentals=0
        ),
        input_output_aliases={len(parts): 0} if target is not None else {},
        compiler_params=pltpu.CompilerParams(vmem_limit_bytes=40 * 1024 * 1024),
        name="combine",
    )(*args)


def shifted(x, axis, size, shift):
    return lax.ppermute(x, axis, [(i, (i + shift) % size) for i in range(size)])


def local(n_tensor, n_section, n_dp, attended, weight_tiles, block_lists, kept_counts, out_grad):
    width = weight_tiles.shape[-1]
    slots = weight_tiles.shape[2]
    rows, in_width = attended.shape[1:]
    row_blocks = in_width // width
    col_blocks = slots // row_blocks
    out_width = col_blocks * width
    total = sum(WEIGHTS)
    edges = [row_blocks * sum(WEIGHTS[:i]) // total for i in range(len(WEIGHTS) + 1)]
    spans = [(a * width, b * width) for a, b in zip(edges, edges[1:]) if b > a]

    own = out_grad[0]
    if n_section == 2:
        other = shifted(own, "section", 2, 1)
        first = lax.axis_index("section") == 0
        columns = jnp.concatenate(
            [jnp.where(first, own, other), jnp.where(first, other, own)], axis=1
        )
    else:
        columns = lax.all_gather(own, "section", axis=1, tiled=True)

    places = block_lists[0, 0]
    numbers = jnp.arange(slots, dtype=jnp.int32)
    slot_of = jnp.sum(
        jnp.where(places[None, :] == numbers[:, None], numbers[None, :], 0), axis=1
    )
    count = kept_counts[0, 0]
    live_of = (slot_of < count).astype(jnp.int32)
    weight = place_tiles(
        weight_tiles[0, 0], jnp.where(live_of > 0, slot_of, 0), live_of, row_blocks, col_blocks
    )

    pieces = [attended[0, :, lo:hi] for lo, hi in spans]
    arrived = []
    for number, piece in enumerate(pieces):
        if number == 1:
            piece, arrived[0] = lax.optimization_barrier((piece, arrived[0]))
        elif number > 1:
            piece, arrived[number - 2] = lax.optimization_barrier((piece, arrived[number - 2]))
        arrived.append(lax.all_gather(piece, "tensor", axis=0))

    length = n_tensor * rows
    partial = None
    mine = []
    sums = jnp.zeros((in_width, out_width), jnp.float32)
    for number, (lo, hi) in enumerate(spans):
        flat = arrived[number].reshape(length, hi - lo)
        grad = lax.dot_general(
            flat, columns, (((0,), (0,)), ((), ())), preferred_element_type=jnp.float32
        ).astype(jnp.bfloat16)
        flat, grad = lax.optimization_barrier((flat, grad))
        summed = grad.astype(jnp.float32)
        for shift in range(1, n_dp):
            summed = summed + shifted(grad, "dp", n_dp, shift).astype(jnp.float32)
        sums = lax.dynamic_update_slice(sums, summed, (lo, 0))
        part = weight[lo:hi]
        if number + 1 < len(spans):
            partial = project(flat, part, partial, jnp.float32, 0, length)
            if number + 2 < len(spans):
                later = number + 1
                arrived[later], partial = lax.optimization_barrier((arrived[later], partial))
        else:
            quarter = length // 4
            mine = [
                project(flat, part, partial, jnp.bfloat16, q * quarter, quarter)
                for q in range(4)
            ]

    projected = None
    for q, own_part in enumerate(mine):
        parts = [own_part] + [
            shifted(own_part, "section", n_section, shift) for shift in range(1, n_section)
        ]
        projected = combine(parts, projected, q * (length // 4), length)

    share = slots // n_dp
    start = lax.axis_index("dp") * share
    mine = lax.dynamic_slice(places, (start,), (share,))
    live = ((start + jnp.arange(share, dtype=jnp.int32)) < count).astype(jnp.int32)
    tiles_grad = pick_blocks(sums, jnp.where(live > 0, mine, 0), live, width)
    return (projected[None], tiles_grad[None, None])


def solution(mesh):
    in_specs = (
        P(("groups", "dp"), "tensor", "section"),
        P("tensor", "section", None, None, None),
        P("tensor", "section", None),
        P("tensor", "section"),
        P(("groups", "dp"), None, ("tensor", "section")),
    )
    out_specs = (
        P(("groups", "dp"), None, "tensor"),
        P(("groups", "tensor"), "section", "dp", None, None),
    )
    body = functools.partial(
        local, mesh.shape["tensor"], mesh.shape["section"], mesh.shape["dp"]
    )
    return jax.shard_map(body, mesh=mesh, in_specs=in_specs, out_specs=out_specs, check_vma=False)
```

time: 602 us -> 485 us (0.81)
  waiting for transfers between devices: 404 us -> 180 us
  Pallas kernels: 0 us -> 151 us
  matrix products: 110 us -> 64.7 us
  local copies, waits for them, and re-layouts: 68.7 us -> 36.9 us
  other arithmetic: 3.23 us -> 27.8 us
    all_gather x2 -> x4, waiting for transfers between devices: 323 us -> 138 us  [local(): arrived.append(lax.all_gather(piece, 'tensor', axis=0))]
    pallas_call x0 -> x13, Pallas kernels: none -> 151 us  [the longest x7 93.7 us: project(): pl.pallas_call(functools.partial(project_kernel, partial is None), grid=(...]
    psum x1 -> x0, waiting for transfers between devices: 50.4 us -> none  [local(): projected = lax.psum(partial_out.astype(jnp.bfloat16), 'section')[None]]
    dot_general x4, matrix products: 110 us -> 64.7 us  [local(): lax.dot_general(flat, columns, (((0,), (0,)), ((), ())), preferred_elemen...]
    ppermute x0 -> x9, waiting for transfers between devices: none -> 42 us  [shifted(): return lax.ppermute(x, axis, [(i, (i + shift) % size) for i in range(size)])]
    unnamed x5 -> x22, local copies, waits for them, and re-layouts: 41.9 us -> 8.98 us
    reduce_scatter x1 -> x0, waiting for transfers between devices: 29.9 us -> none  [local(): lax.psum_scatter(tile_sum.astype(jnp.bfloat16), 'dp', scatter_dimension=0...]
    transpose x2 -> x0, local copies, waits for them, and re-layouts: 17.8 us -> none  [local(): jnp.transpose(blocks, (0, 2, 1, 3))]
  transfers between devices with their start and end apart: 4 -> 13, of which waited for: 4 -> 6; matrix products, arithmetic and copies ran while one was open for 13% -> 24% of each run, Pallas kernels for 0% -> 30%
where the time goes in v1:
time: 485 us; the launch traced here: 481 us
  waiting for transfers between devices  180 us (37%)
  Pallas kernels  151 us (31%)
  matrix products  64.7 us (13%)
  local copies, waits for them, and re-layouts  36.9 us (8%)
  other arithmetic  27.8 us (6%)
  between operations  14.5 us (3%)
  starting transfers between devices  6.2 us (1%)
    all_gather x4, waiting for transfers between devices, local(): arrived.append(lax.all_gather(piece, 'tensor', axis=0))  138 us
    pallas_call x7, Pallas kernels, project(): pl.pallas_call(functools.partial(project_kernel, partial is None), grid=(...  93.7 us
    dot_general x4, matrix products, local(): lax.dot_general(flat, columns, (((0,), (0,)), ((), ())), preferred_elemen...  64.7 us
    ppermute x9, waiting for transfers between devices, shifted(): return lax.ppermute(x, axis, [(i, (i + shift) % size) for i in range(size)])  42 us
    pallas_call x4, Pallas kernels, combine(): pl.pallas_call(functools.partial(combine_kernel, len(parts)), grid=(heigh...  24.1 us
    pallas_call x1, Pallas kernels, place_tiles(): pl.pallas_call(functools.partial(place_kernel, count), grid_spec=pltpu.Pr...  20.3 us
    pallas_call x1, Pallas kernels, pick_blocks(): pl.pallas_call(functools.partial(pick_kernel, count), grid_spec=pltpu.Pre...  12.7 us
    select_n x1, other arithmetic, local(): jnp.where(first, own, other)  11.5 us
  transfers between devices with their start and end apart: 13, of which 6 were waited for; matrix products, arithmetic and copies ran while one was open for 24% of the time, Pallas kernels for 30%

profile of v1, /device:TPU:0, one launch (start us, length us, event | category | flops | bytes accessed | tf_op | source)
XLA Modules:
  0.0 481.0 jit_solution(8280470164175286573)
XLA Ops:
  7.2 2.7 slice.26
  10.5 2.5 slice_bitcast_fusion
  13.0 115.3 %all-gather.8.cloned.1.call-done = bf16[4,1024,768]{2,1,0:T(8,128)(2,1)} async-done(((bf16[1,1024,768]{2,1,0:T(8,128)(2,1)}), bf16[4,1024,768]{2,1,0:T(8,128)(2,1)}) %all-gather.8.cloned.1.call-update) | async-done | bytes 6291472 | tf_op jit(solution)/shard_map/all_gather | solution.py:216
  129.1 0.6 compare_select_fusion.1.slot_ref
  129.7 0.5 compare_convert_fusion.1.live_ref
  130.2 20.3 %place.1 = bf16[2048,2048]{1,0:T(8,128)(2,1)} custom-call(s32[256]{0:T(256)} %compare_select_fusion.1.slot_ref, s32[256]{0:T(256)} %compare_convert_fusion.1.live_ref, bf16[256,128,128]{2,1,0:T(8,128)(2,1)} %bitcast.32, bf16[256,128,128]{2,1,0:T(8,128)(2,1)} %bitcast.33, bf16[256,128,128]{2,1,0:T(8,128)(2,1)} %bitcast.34, bf16[256,128,128]{2,1,0:T(8,128)(2,1)} %bitcast.35, ...), custom_call_target="tpu_custom_call" | custom-call | bytes 16777216 | tf_op jit(solution)/shard_map/place/pallas_call | solution.py:38
  150.5 1.3 slice.32.weight_ref
  151.8 4.0 slice.33.weight_ref
  155.8 3.6 slice.34.weight_ref
  159.4 1.5 slice.35.weight_ref
  160.9 1.9 slice_bitcast_fusion.2
  162.8 2.1 slice_bitcast_fusion.1
  165.0 11.5 %broadcast_select_fusion.1 = (bf16[4096,1024]{1,0:T(8,128)(2,1)}, bf16[4096,1024]{1,0:T(8,128)(2,1)}) fusion(bf16[4096,1024]{1,0:T(8,128)(2,1)} %collective-permute-done, pred[]{:T(512)S(6)} %eq.18, bf16[1,4096,1024]{2,1,0:T(8,128)(2,1)} %param.9), kind=kLoop, calls=%fused_computation.2 | loop fusion | flops 8388608 | bytes 33554432 | tf_op jit(solution)/shard_map/jit(_where)/select_n | solution.py:193
  176.5 20.1 %convolution_convert_fusion = bf16[768,2048]{1,0:T(8,128)(2,1)} fusion(bf16[4096,768]{1,0:T(8,128)(2,1)} %bitcast.30, bf16[4096,1024]{1,0:T(8,128)(2,1)} %get-tuple-element.41, bf16[4096,1024]{1,0:T(8,128)(2,1)} %get-tuple-element.40), kind=kOutput, calls=%fused_computation.5 | convolution fusion | flops 12920029184 | bytes 26214400 | tf_op jit(solution)/shard_map/dot_general | solution.py:224
  196.6 1.4 collective-permute-start.5
  198.1 1.9 copy-done.4
  200.0 2.8 copy-done.5
  202.8 16.9 %project.7.refs_0_ = f32[4096,2048]{1,0:T(8,128)} custom-call(bf16[4096,768]{1,0:T(8,128)(2,1)S(1)} %bitcast.31, bf16[768,2048]{1,0:T(8,128)(2,1)S(1)} %copy-done.4), custom_call_target="tpu_custom_call" | custom-call | flops 12884901888 | bytes 76546048 | tf_op jit(solution)/shard_map/project/pallas_call | solution.py:125
  219.7 6.4 %all-gather.10.cloned.1.call-done = bf16[4096,640]{1,0:T(8,128)(2,1)} async-done(((bf16[1024,640]{1,0:T(8,128)(2,1)}), bf16[4096,640]{1,0:T(8,128)(2,1)}) %all-gather.10.cloned.1.call-update) | async-done | bytes 5242896 | tf_op jit(solution)/shard_map/all_gather | solution.py:216
  226.2 17.6 %convolution_convert_fusion.1 = bf16[640,2048]{1,0:T(8,128)(2,1)} fusion(bf16[4096,640]{1,0:T(8,128)(2,1)} %all-gather.10.cloned.1.call-done, bf16[4096,1024]{1,0:T(8,128)(2,1)} %get-tuple-element.41, bf16[4096,1024]{1,0:T(8,128)(2,1)} %get-tuple-element.40), kind=kOutput, calls=%fused_computation.6 | convolution fusion | flops 10772283392 | bytes 24641536 | tf_op jit(solution)/shard_map/dot_general | solution.py:224
  243.8 1.8 copy-done.1
  245.5 2.5 copy-done.2
  248.0 28.5 %project.8.refs_0_ = f32[4096,2048]{1,0:T(8,128)} custom-call(bf16[4096,640]{1,0:T(8,128)(2,1)S(1)} %copy-done.2, bf16[640,2048]{1,0:T(8,128)(2,1)S(1)} %copy-done.1, f32[4096,2048]{1,0:T(8,128)} %project.7.refs_0_), custom_call_target="tpu_custom_call", output_to_operand_aliasing={{}: (2, {})} | custom-call | flops 10737418240 | bytes 74973184 | tf_op jit(solution)/shard_map/project/pallas_call | solution.py:125
  276.6 13.0 %all-gather.14.cloned.1.call-done = bf16[4096,384]{1,0:T(8,128)(2,1)} async-done(((bf16[1024,384]{1,0:T(8,128)(2,1)}), bf16[4096,384]{1,0:T(8,128)(2,1)}) %all-gather.14.cloned.1.call-update) | async-done | bytes 3145744 | tf_op jit(solution)/shard_map/all_gather | solution.py:216
  289.6 14.9 %convolution_convert_fusion.2 = bf16[384,2048]{1,0:T(8,128)(2,1)} fusion(bf16[4096,384]{1,0:T(8,128)(2,1)} %all-gather.14.cloned.1.call-done, bf16[4096,1024]{1,0:T(8,128)(2,1)} %get-tuple-element.41, bf16[4096,1024]{1,0:T(8,128)(2,1)} %get-tuple-element.40), kind=kOutput, calls=%fused_computation.8 | convolution fusion | flops 6476791808 | bytes 21495808 | tf_op jit(solution)/shard_map/dot_general | solution.py:224
  304.5 1.4 collective-permute-start.6
  305.9 0.6 collective-permute-start.7
  306.5 25.9 %project.9.refs_0_ = f32[4096,2048]{1,0:T(8,128)} custom-call(bf16[4096,384]{1,0:T(8,128)(2,1)S(1)} %copy-done.3, bf16[384,2048]{1,0:T(8,128)(2,1)S(1)} %slice.35.weight_ref, f32[4096,2048]{1,0:T(8,128)} %project.8.refs_0_), custom_call_target="tpu_custom_call", output_to_operand_aliasing={{}: (2, {})} | custom-call | flops 6442450944 | bytes 71827456 | tf_op jit(solution)/shard_map/project/pallas_call | solution.py:125
  332.4 3.3 all-gather.12.cloned.1.call-done.rows_ref
  335.7 12.0 %convolution_convert_fusion.3 = bf16[256,2048]{1,0:T(8,128)(2,1)} fusion(bf16[4096,256]{1,0:T(8,128)(2,1)} %all-gather.12.cloned.1.call-done.rows_ref, bf16[4096,1024]{1,0:T(8,128)(2,1)} %get-tuple-element.41, bf16[4096,1024]{1,0:T(8,128)(2,1)} %get-tuple-element.40), kind=kOutput, calls=%fused_computation.9 | convolution fusion | flops 4329046016 | bytes 19922944 | tf_op jit(solution)/shard_map/dot_general | solution.py:224
  347.7 5.5 %project.13.refs_0_ = bf16[1024,2048]{1,0:T(8,128)(2,1)} custom-call(bf16[4096,256]{1,0:T(8,128)(2,1)S(1)} %copy-done, bf16[256,2048]{1,0:T(8,128)(2,1)S(1)} %slice.32.weight_ref, f32[4096,2048]{1,0:T(8,128)} %project.9.refs_0_), custom_call_target="tpu_custom_call" | custom-call | flops 1073741824 | bytes 18350080 | tf_op jit(solution)/shard_map/project/pallas_call | solution.py:125
  353.2 5.6 %project.10.refs_0_ = bf16[1024,2048]{1,0:T(8,128)(2,1)} custom-call(bf16[4096,256]{1,0:T(8,128)(2,1)S(1)} %copy-done, bf16[256,2048]{1,0:T(8,128)(2,1)S(1)} %slice.32.weight_ref, f32[4096,2048]{1,0:T(8,128)} %project.9.refs_0_), custom_call_target="tpu_custom_call" | custom-call | flops 1073741824 | bytes 18350080 | tf_op jit(solution)/shard_map/project/pallas_call | solution.py:125
  358.8 5.6 %project.11.refs_0_ = bf16[1024,2048]{1,0:T(8,128)(2,1)} custom-call(bf16[4096,256]{1,0:T(8,128)(2,1)S(1)} %copy-done, bf16[256,2048]{1,0:T(8,128)(2,1)S(1)} %slice.32.weight_ref, f32[4096,2048]{1,0:T(8,128)} %project.9.refs_0_), custom_call_target="tpu_custom_call" | custom-call | flops 1073741824 | bytes 18350080 | tf_op jit(solution)/shard_map/project/pallas_call | solution.py:125
  364.4 5.6 %project.12.refs_0_ = bf16[1024,2048]{1,0:T(8,128)(2,1)} custom-call(bf16[4096,256]{1,0:T(8,128)(2,1)S(1)} %copy-done, bf16[256,2048]{1,0:T(8,128)(2,1)S(1)} %slice.32.weight_ref, f32[4096,2048]{1,0:T(8,128)} %project.9.refs_0_), custom_call_target="tpu_custom_call" | custom-call | flops 1073741824 | bytes 18350080 | tf_op jit(solution)/shard_map/project/pallas_call | solution.py:125
  370.6 26.4 %collective-permute-done.7 = bf16[384,2048]{1,0:T(8,128)(2,1)} collective-permute-done((bf16[384,2048]{1,0:T(8,128)(2,1)}, bf16[384,2048]{1,0:T(8,128)(2,1)}, u32[]{:S(2)}, u32[]{:S(2)}) %collective-permute-start.7) | collective-permute-done | bytes 1572896 | tf_op jit(solution)/shard_map/ppermute | solution.py:174
  397.0 0.6 compare_select_fusion
  397.6 4.2 convert_add_fusion
  401.7 8.4 %dynamic_update_slice.12 = f32[2048,2048]{1,0:T(8,128)} pad(f32[768,2048]{1,0:T(8,128)S(1)} %convert_add_fusion, f32[]{:T(128)} %constant.5.clone.1), padding=0_1280x0_0 | pad | bytes 23068676 | tf_op jit(solution)/shard_map/dynamic_update_slice | solution.py:231
  410.1 1.5 collective-permute-start.8
  411.6 5.1 %add_dynamic-update-slice_fusion = f32[2048,2048]{1,0:T(8,128)} fusion(f32[2048,2048]{1,0:T(8,128)} %dynamic_update_slice.12, bf16[640,2048]{1,0:T(8,128)(2,1)} %collective-permute-done.6, bf16[640,2048]{1,0:T(8,128)(2,1)S(1)} %copy-done.6), kind=kLoop, calls=%fused_computation.4 | loop fusion | flops 3932160 | bytes 10485760 | tf_op jit(solution)/shard_map/dynamic_update_slice | solution.py:231
  416.7 3.6 add_dynamic-update-slice_fusion.1
  420.3 15.6 %collective-permute-done.8 = bf16[256,2048]{1,0:T(8,128)(2,1)S(1)} collective-permute-done((bf16[256,2048]{1,0:T(8,128)(2,1)}, bf16[256,2048]{1,0:T(8,128)(2,1)S(1)}, u32[]{:S(2)}, u32[]{:S(2)}) %collective-permute-start.8) | collective-permute-done | bytes 1048608 | tf_op jit(solution)/shard_map/ppermute | solution.py:174
  435.9 1.7 add_dynamic-update-slice_fusion.2.refs_0_.refs_1_.refs_2_.refs_3_.refs_4_.refs_5_.refs_6_.refs_7_
  437.6 12.7 %pick.1 = f32[128,128,128]{2,1,0:T(8,128)} custom-call(s32[128]{0:T(128)} %get-tuple-element.38.block_ref, s32[128]{0:T(128)} %get-tuple-element.39.live_ref, f32[2048,2048]{1,0:T(8,128)} %add_dynamic-update-slice_fusion.2.refs_0_.refs_1_.refs_2_.refs_3_.refs_4_.refs_5_.refs_6_.refs_7_, ...), custom_call_target="tpu_custom_call" | custom-call | bytes 16777216 | tf_op jit(solution)/shard_map/pick/pallas_call | solution.py:85
  450.3 6.0 %combine.4.refs_2_ = bf16[4096,2048]{1,0:T(8,128)(2,1)} custom-call(bf16[1024,2048]{1,0:T(8,128)(2,1)} %project.13.refs_0_, bf16[1024,2048]{1,0:T(8,128)(2,1)} %collective-permute-done.4.refs_1_), custom_call_target="tpu_custom_call" | custom-call | bytes 12582912 | tf_op jit(solution)/shard_map/combine/pallas_call | solution.py:158
  456.4 6.0 %combine.5.refs_2_ = bf16[4096,2048]{1,0:T(8,128)(2,1)} custom-call(bf16[1024,2048]{1,0:T(8,128)(2,1)} %project.12.refs_0_, bf16[1024,2048]{1,0:T(8,128)(2,1)} %collective-permute-done.3.refs_1_, bf16[4096,2048]{1,0:T(8,128)(2,1)} %combine.4.refs_2_), custom_call_target="tpu_custom_call", output_to_operand_aliasing={{}: (2, {})} | custom-call | bytes 12582912 | tf_op jit(solution)/shard_map/combine/pallas_call | solution.py:158
  462.4 6.0 %combine.6.refs_2_ = bf16[4096,2048]{1,0:T(8,128)(2,1)} custom-call(bf16[1024,2048]{1,0:T(8,128)(2,1)} %project.11.refs_0_, bf16[1024,2048]{1,0:T(8,128)(2,1)} %collective-permute-done.2.refs_1_, bf16[4096,2048]{1,0:T(8,128)(2,1)} %combine.5.refs_2_), custom_call_target="tpu_custom_call", output_to_operand_aliasing={{}: (2, {})} | custom-call | bytes 12582912 | tf_op jit(solution)/shard_map/combine/pallas_call | solution.py:158
  468.4 6.0 %combine.7 = bf16[4096,2048]{1,0:T(8,128)(2,1)} custom-call(bf16[1024,2048]{1,0:T(8,128)(2,1)} %project.10.refs_0_, bf16[1024,2048]{1,0:T(8,128)(2,1)} %collective-permute-done.1.refs_1_, bf16[4096,2048]{1,0:T(8,128)(2,1)} %combine.6.refs_2_), custom_call_target="tpu_custom_call", output_to_operand_aliasing={{}: (2, {})} | custom-call | bytes 12582912 | tf_op jit(solution)/shard_map/combine/pallas_call | solution.py:158
  (39 shorter events, 1.5 us)
Async XLA Ops:
  7.2 121.8 %copy-start.9 = (s32[1,1,256]{2,1,0:T(1,128)S(1)}, s32[1,1,256]{2,1,0:T(1,128)}, u32[]{:S(2)}) copy-start(s32[1,1,256]{2,1,0:T(1,128)} %param.7) | copy-start | bytes 3076
  7.2 121.1 %all-gather.8.cloned.1.call-start = ((), (), s32[]{:S(2)}) async-start(), calls=%async_computation | async-start | bytes 7864320 | tf_op jit(solution)/shard_map/all_gather | solution.py:216
  9.9 216.2 %all-gather.10.cloned.1.call-start = ((), (), s32[]{:S(2)}) async-start(), calls=%async_computation.1 | async-start | bytes 6553600 | tf_op jit(solution)/shard_map/all_gather | solution.py:216
  9.9 155.0 %collective-permute-start = (bf16[4096,1024]{1,0:T(8,128)(2,1)}, bf16[4096,1024]{1,0:T(8,128)(2,1)}, u32[]{:S(2)}, u32[]{:S(2)}) collective-permute-start(bf16[4096,1024]{1,0:T(8,128)(2,1)} %bitcast.41), channel_id=1, source_target_pairs={{0,1},{1,0},{2,3},{3,2},{4,5},{5,4},{6,7},{7,6},{8,9},{9,8},{10,11... | collective-permute-start | bytes 25165832 | tf_op jit(solution)/shard_map/ppermute | solution.py:174
  128.3 161.4 %all-gather.14.cloned.1.call-start = ((), (), s32[]{:S(2)}) async-start(), calls=%async_computation.3 | async-start | bytes 3932160 | tf_op jit(solution)/shard_map/all_gather | solution.py:216
  164.9 170.7 %all-gather.12.cloned.1.call-start = ((), (), s32[]{:S(2)}) async-start(), calls=%async_computation.2 | async-start | bytes 2621440 | tf_op jit(solution)/shard_map/all_gather | solution.py:216
  196.6 173.9 %collective-permute-start.5 = (bf16[768,2048]{1,0:T(8,128)(2,1)}, bf16[768,2048]{1,0:T(8,128)(2,1)}, u32[]{:S(2)}, u32[]{:S(2)}) collective-permute-start(bf16[768,2048]{1,0:T(8,128)(2,1)} %convolution_convert_fusion), channel_id=1, source_target_pairs={{0,2},{2,0},{1,3},{3,1},{4,6},{6,4},{5,7},{7,5},{8,10},{10,8},{9,1... | collective-permute-start | bytes 9437192 | tf_op jit(solution)/shard_map/ppermute | solution.py:174
  198.1 1.9 copy-start.4
  200.0 2.8 copy-start.5
  243.8 1.8 copy-start.1
  245.5 2.5 copy-start.2
  289.6 16.9 %copy-start.3 = (bf16[4096,384]{1,0:T(8,128)(2,1)S(1)}, bf16[4096,384]{1,0:T(8,128)(2,1)}, u32[]{:S(2)}) copy-start(bf16[4096,384]{1,0:T(8,128)(2,1)} %all-gather.14.cloned.1.call-done) | copy-start | bytes 9437188
  304.5 105.6 %collective-permute-start.6 = (bf16[640,2048]{1,0:T(8,128)(2,1)}, bf16[640,2048]{1,0:T(8,128)(2,1)}, u32[]{:S(2)}, u32[]{:S(2)}) collective-permute-start(bf16[640,2048]{1,0:T(8,128)(2,1)} %convolution_convert_fusion.1), channel_id=1, source_target_pairs={{0,2},{2,0},{1,3},{3,1},{4,6},{6,4},{5,7},{7,5},{8,10},{10,8},{9,1... | collective-permute-start | bytes 7864328 | tf_op jit(solution)/shard_map/ppermute | solution.py:174
  305.9 91.1 %collective-permute-start.7 = (bf16[384,2048]{1,0:T(8,128)(2,1)}, bf16[384,2048]{1,0:T(8,128)(2,1)}, u32[]{:S(2)}, u32[]{:S(2)}) collective-permute-start(bf16[384,2048]{1,0:T(8,128)(2,1)} %convolution_convert_fusion.2), channel_id=1, source_target_pairs={{0,2},{2,0},{1,3},{3,1},{4,6},{6,4},{5,7},{7,5},{8,10},{10,8},{9,1... | collective-permute-start | bytes 4718600 | tf_op jit(solution)/shard_map/ppermute | solution.py:174
  335.7 12.0 %copy-start = (bf16[4096,256]{1,0:T(8,128)(2,1)S(1)}, bf16[4096,256]{1,0:T(8,128)(2,1)}, u32[]{:S(2)}) copy-start(bf16[4096,256]{1,0:T(8,128)(2,1)} %all-gather.12.cloned.1.call-done.rows_ref) | copy-start | bytes 6291460
  353.2 97.1 %collective-permute-start.4 = (bf16[1024,2048]{1,0:T(8,128)(2,1)}, bf16[1024,2048]{1,0:T(8,128)(2,1)}, u32[]{:S(2)}, u32[]{:S(2)}) collective-permute-start(bf16[1024,2048]{1,0:T(8,128)(2,1)} %project.13.refs_0_), channel_id=1, source_target_pairs={{0,1},{1,0},{2,3},{3,2},{4,5},{5,4},{6,7},{7,6},{8,9},{9,8},{10,11... | collective-permute-start | bytes 12582920 | tf_op jit(solution)/shard_map/ppermute | solution.py:174
  364.4 32.6 %copy-start.10 = (s32[1,1,256]{2,1,0:T(1,128)S(1)}, s32[1,1,256]{2,1,0:T(1,128)}, u32[]{:S(2)}) copy-start(s32[1,1,256]{2,1,0:T(1,128)} %param.7) | copy-start | bytes 3076
  370.0 86.4 %collective-permute-start.3 = (bf16[1024,2048]{1,0:T(8,128)(2,1)}, bf16[1024,2048]{1,0:T(8,128)(2,1)}, u32[]{:S(2)}, u32[]{:S(2)}) collective-permute-start(bf16[1024,2048]{1,0:T(8,128)(2,1)} %project.12.refs_0_), channel_id=1, source_target_pairs={{0,1},{1,0},{2,3},{3,2},{4,5},{5,4},{6,7},{7,6},{8,9},{9,8},{10,11... | collective-permute-start | bytes 12582920 | tf_op jit(solution)/shard_map/ppermute | solution.py:174
  370.5 91.9 %collective-permute-start.2 = (bf16[1024,2048]{1,0:T(8,128)(2,1)}, bf16[1024,2048]{1,0:T(8,128)(2,1)}, u32[]{:S(2)}, u32[]{:S(2)}) collective-permute-start(bf16[1024,2048]{1,0:T(8,128)(2,1)} %project.11.refs_0_), channel_id=1, source_target_pairs={{0,1},{1,0},{2,3},{3,2},{4,5},{5,4},{6,7},{7,6},{8,9},{9,8},{10,11... | collective-permute-start | bytes 12582920 | tf_op jit(solution)/shard_map/ppermute | solution.py:174
  397.0 71.4 %collective-permute-start.1 = (bf16[1024,2048]{1,0:T(8,128)(2,1)}, bf16[1024,2048]{1,0:T(8,128)(2,1)}, u32[]{:S(2)}, u32[]{:S(2)}) collective-permute-start(bf16[1024,2048]{1,0:T(8,128)(2,1)} %project.10.refs_0_), channel_id=1, source_target_pairs={{0,1},{1,0},{2,3},{3,2},{4,5},{5,4},{6,7},{7,6},{8,9},{9,8},{10,11... | collective-permute-start | bytes 12582920 | tf_op jit(solution)/shard_map/ppermute | solution.py:174
  401.7 9.9 %copy-start.6 = (bf16[640,2048]{1,0:T(8,128)(2,1)S(1)}, bf16[640,2048]{1,0:T(8,128)(2,1)}, u32[]{:S(2)}) copy-start(bf16[640,2048]{1,0:T(8,128)(2,1)} %convolution_convert_fusion.1) | copy-start | bytes 7864324
  410.1 6.6 %copy-start.7 = (bf16[384,2048]{1,0:T(8,128)(2,1)S(1)}, bf16[384,2048]{1,0:T(8,128)(2,1)}, u32[]{:S(2)}) copy-start(bf16[384,2048]{1,0:T(8,128)(2,1)} %convolution_convert_fusion.2) | copy-start | bytes 4718596
  410.1 25.8 %copy-start.8 = (bf16[256,2048]{1,0:T(8,128)(2,1)S(1)}, bf16[256,2048]{1,0:T(8,128)(2,1)}, u32[]{:S(2)}) copy-start(bf16[256,2048]{1,0:T(8,128)(2,1)} %convolution_convert_fusion.3) | copy-start | bytes 3145732
  410.1 25.8 %collective-permute-start.8 = (bf16[256,2048]{1,0:T(8,128)(2,1)}, bf16[256,2048]{1,0:T(8,128)(2,1)S(1)}, u32[]{:S(2)}, u32[]{:S(2)}) collective-permute-start(bf16[256,2048]{1,0:T(8,128)(2,1)} %convolution_convert_fusion.3), channel_id=1, source_target_pairs={{0,2},{2,0},{1,3},{3,1},{4,6},{6,4},{5,7},{7,5},{8,10},{10,8},{9,1... | collective-permute-start | bytes 3145736 | tf_op jit(solution)/shard_map/ppermute | solution.py:174
Sparse Core Ops, SparseCore 0:
  10.2 118.0 all-gather.7
  129.8 96.2 all-gather.9
  227.7 61.8 all-gather.13
  291.0 44.5 all-gather.11

commit v2 on v1

--- a/solution.py
+++ b/solution.py
@@ -1,4 +1,5 @@
 import functools
+import math
 
 import jax
 import jax.numpy as jnp
@@ -7,15 +8,16 @@
 from jax.experimental.pallas import tpu as pltpu
 from jax.sharding import PartitionSpec as P
 
-WEIGHTS = (6, 5, 3, 2)
-
-
-def place_kernel(count, slot_ref, live_ref, *refs):
+WEIGHTS = (5, 5, 4, 2)
+SMALL = pl.CostEstimate(flops=0, bytes_accessed=1024, transcendentals=0)
+
+
+def place_kernel(count, first, slot_ref, live_ref, *refs):
     tiles, out = refs[:count], refs[count]
     width = tiles[0].shape[-1]
     step = pl.program_id(0)
     for u in range(count):
-        live = live_ref[step * count + u] > 0
+        live = live_ref[first + step * count + u] > 0
         columns = slice(u * width, (u + 1) * width)
 
         @pl.when(live)
@@ -27,16 +29,17 @@
             out[:, columns] = jnp.zeros_like(tiles[u][0])
 
 
-def place_tiles(tiles, slot_of, live_of, row_blocks, col_blocks):
+def place_tiles(tiles, slot_of, live_of, row_begin, row_blocks, col_blocks):
     width = tiles.shape[-1]
     count = min(8, col_blocks)
     groups = col_blocks // count
+    first = row_begin * col_blocks
 
     def tile_map(u, i, slot_ref, live_ref):
-        return (slot_ref[i * count + u], 0, 0)
-
-    return pl.pallas_call(
-        functools.partial(place_kernel, count),
+        return (slot_ref[first + i * count + u], 0, 0)
+
+    return pl.pallas_call(
+        functools.partial(place_kernel, count, first),
         grid_spec=pltpu.PrefetchScalarGridSpec(
             num_scalar_prefetch=2,
             grid=(row_blocks * groups,),
@@ -51,9 +54,7 @@
         out_shape=jax.ShapeDtypeStruct(
             (row_blocks * width, col_blocks * width), tiles.dtype
         ),
-        cost_estimate=pl.CostEstimate(
-            flops=0, bytes_accessed=4 * tiles.size, transcendentals=0
-        ),
+        cost_estimate=SMALL,
         name="place",
     )(slot_of, live_of, *([tiles] * count))
 
@@ -94,9 +95,7 @@
             out_specs=pl.BlockSpec((count, width, width), lambda i, b, l: (i, 0, 0)),
         ),
         out_shape=jax.ShapeDtypeStruct((slots, width, width), dense.dtype),
-        cost_estimate=pl.CostEstimate(
-            flops=0, bytes_accessed=8 * slots * width * width, transcendentals=0
-        ),
+        cost_estimate=SMALL,
         name="pick",
     )(block_of, live_of, *([dense] * count))
 
@@ -121,16 +120,18 @@
     if partial is not None:
         specs.append(pl.BlockSpec((block, width), lambda i: (offset + i, 0)))
         args.append(partial)
-    moved = (height * depth + depth * width) * 2 + height * width * 8
+    cost = pl.CostEstimate(
+        flops=2 * height * depth * width,
+        bytes_accessed=(height * depth + depth * width) * 2 + height * width * 8,
+        transcendentals=0,
+    )
     return pl.pallas_call(
         functools.partial(project_kernel, partial is None),
         grid=(height // block,),
         in_specs=specs,
         out_specs=pl.BlockSpec((block, width), lambda i: (i, 0)),
         out_shape=jax.ShapeDtypeStruct((height, width), dtype),
-        cost_estimate=pl.CostEstimate(
-            flops=2 * height * depth * width, bytes_accessed=moved, transcendentals=0
-        ),
+        cost_estimate=SMALL,
         input_output_aliases=(
             {2: 0} if partial is not None and partial.dtype == dtype else {}
         ),
@@ -146,9 +147,9 @@
     refs[-1][...] = total.astype(refs[-1].dtype)
 
 
-def combine(parts, target, begin, length):
+def combine(parts, target, begin, length, dtype):
     height, width = parts[0].shape
-    block = min(256, height)
+    block = math.gcd(math.gcd(256, height), begin)
     offset = begin // block
     specs = [pl.BlockSpec((block, width), lambda i: (i, 0))] * len(parts)
     args = list(parts)
@@ -160,10 +161,8 @@
         grid=(height // block,),
         in_specs=specs,
         out_specs=pl.BlockSpec((block, width), lambda i: (offset + i, 0)),
-        out_shape=jax.ShapeDtypeStruct((length, width), parts[0].dtype),
-        cost_estimate=pl.CostEstimate(
-            flops=0, bytes_accessed=6 * height * width, transcendentals=0
-        ),
+        out_shape=jax.ShapeDtypeStruct((length, width), dtype),
+        cost_estimate=SMALL,
         input_output_aliases={len(parts): 0} if target is not None else {},
         compiler_params=pltpu.CompilerParams(vmem_limit_bytes=40 * 1024 * 1024),
         name="combine",
@@ -202,9 +201,13 @@
     )
     count = kept_counts[0, 0]
     live_of = (slot_of < count).astype(jnp.int32)
-    weight = place_tiles(
-        weight_tiles[0, 0], jnp.where(live_of > 0, slot_of, 0), live_of, row_blocks, col_blocks
-    )
+    placed_slot = jnp.where(live_of > 0, slot_of, 0)
+    weights = [
+        place_tiles(
+            weight_tiles[0, 0], placed_slot, live_of, lo // width, (hi - lo) // width, col_blocks
+        )
+        for lo, hi in spans
+    ]
 
     pieces = [attended[0, :, lo:hi] for lo, hi in spans]
     arrived = []
@@ -218,18 +221,18 @@
     length = n_tensor * rows
     partial = None
     mine = []
-    sums = jnp.zeros((in_width, out_width), jnp.float32)
+    sums = None
     for number, (lo, hi) in enumerate(spans):
         flat = arrived[number].reshape(length, hi - lo)
         grad = lax.dot_general(
             flat, columns, (((0,), (0,)), ((), ())), preferred_element_type=jnp.float32
         ).astype(jnp.bfloat16)
         flat, grad = lax.optimization_barrier((flat, grad))
-        summed = grad.astype(jnp.float32)
-        for shift in range(1, n_dp):
-            summed = summed + shifted(grad, "dp", n_dp, shift).astype(jnp.float32)
-        sums = lax.dynamic_update_slice(sums, summed, (lo, 0))
-        part = weight[lo:hi]
+        parts = [grad] + [shifted(grad, "dp", n_dp, shift) for shift in range(1, n_dp)]
+        sums = combine(parts, sums, lo, in_width, jnp.float32)
+        if number == len(spans) - 3:
+            arrived[-1], sums = lax.optimization_barrier((arrived[-1], sums))
+        part = weights[number]
         if number + 1 < len(spans):
             partial = project(flat, part, partial, jnp.float32, 0, length)
             if number + 2 < len(spans):
@@ -247,7 +250,7 @@
         parts = [own_part] + [
             shifted(own_part, "section", n_section, shift) for shift in range(1, n_section)
         ]
-        projected = combine(parts, projected, q * (length // 4), length)
+        projected = combine(parts, projected, q * (length // 4), length, jnp.bfloat16)
 
     share = slots // n_dp
     start = lax.axis_index("dp") * share

time: 485 us -> 499 us (1.029)
  waiting for transfers between devices: 180 us -> 207 us
  Pallas kernels: 151 us -> 172 us
  local copies, waits for them, and re-layouts: 36.9 us -> 17.9 us
  other arithmetic: 27.8 us -> 13.3 us
    ppermute x9, waiting for transfers between devices: 42 us -> 64.6 us  [shifted(): return lax.ppermute(x, axis, [(i, (i + shift) % size) for i in range(size)])]
    pallas_call x4 -> x8, Pallas kernels: 24.1 us -> 41 us  [combine(): pl.pallas_call(functools.partial(combine_kernel, len(parts)), grid=(heigh...]
    slice x4 -> x0, local copies, waits for them, and re-layouts: 10.4 us -> none  [local(): part = weight[lo:hi]]
    dynamic_update_slice x3 -> x0, other arithmetic: 10.4 us -> none  [local(): sums = lax.dynamic_update_slice(sums, summed, (lo, 0))]
    dynamic_update_slice x1 -> x0, local copies, waits for them, and re-layouts: 8.38 us -> none  [local(): sums = lax.dynamic_update_slice(sums, summed, (lo, 0))]
    pallas_call x1 -> x4, Pallas kernels: 20.3 us -> 25.6 us  [place_tiles(): pl.pallas_call(functools.partial(place_kernel, count, first), grid_spec=p...]
    unnamed x22 -> x28, local copies, waits for them, and re-layouts: 8.98 us -> 10.2 us
  transfers between devices with their start and end apart: 13 -> 13, of which waited for: 6 -> 5; matrix products, arithmetic and copies ran while one was open for 24% -> 14% of each run, Pallas kernels for 30% -> 32%
where the time goes in v2:
time: 499 us; the launch traced here: 495 us
  waiting for transfers between devices  207 us (41%)
  Pallas kernels  172 us (34%)
  matrix products  64 us (13%)
  local copies, waits for them, and re-layouts  17.9 us (4%)
  between operations  14.5 us (3%)
  other arithmetic  13.3 us (3%)
  starting transfers between devices  7.09 us (1%)
    all_gather x4, waiting for transfers between devices, local(): arrived.append(lax.all_gather(piece, 'tensor', axis=0))  142 us
    pallas_call x7, Pallas kernels, project(): pl.pallas_call(functools.partial(project_kernel, partial is None), grid=(...  93.7 us
    ppermute x9, waiting for transfers between devices, shifted(): return lax.ppermute(x, axis, [(i, (i + shift) % size) for i in range(size)])  64.6 us
    dot_general x4, matrix products, local(): lax.dot_general(flat, columns, (((0,), (0,)), ((), ())), preferred_elemen...  64 us
    pallas_call x8, Pallas kernels, combine(): pl.pallas_call(functools.partial(combine_kernel, len(parts)), grid=(heigh...  41 us
    pallas_call x4, Pallas kernels, place_tiles(): pl.pallas_call(functools.partial(place_kernel, count, first), grid_spec=p...  25.6 us
    pallas_call x1, Pallas kernels, pick_blocks(): pl.pallas_call(functools.partial(pick_kernel, count), grid_spec=pltpu.Pre...  11.5 us
    select_n x1, other arithmetic, local(): jnp.where(first, own, other)  11.5 us
  transfers between devices with their start and end apart: 13, of which 5 were waited for; matrix products, arithmetic and copies ran while one was open for 14% of the time, Pallas kernels for 32%

profile of v2, /device:TPU:0, one launch (start us, length us, event | category | flops | bytes accessed | tf_op | source)
XLA Modules:
  0.0 495.3 jit_solution(15551731374781737998)
XLA Ops:
  7.2 3.5 fusion
  10.8 100.9 %all-gather.8.cloned.1.call-done = bf16[4,1024,640]{2,1,0:T(8,128)(2,1)} async-done(((bf16[1,1024,640]{2,1,0:T(8,128)(2,1)}), bf16[4,1024,640]{2,1,0:T(8,128)(2,1)}) %all-gather.8.cloned.1.call-update) | async-done | bytes 5242896 | tf_op jit(solution)/shard_map/all_gather | solution.py:219
  111.8 2.3 slice_bitcast_fusion.1
  114.9 0.1 select_reduce_fusion
  115.0 0.6 compare_convert_fusion.1.live_ref
  115.6 0.6 compare_select_fusion.1.slot_ref
  116.2 7.5 %place.4.weight_ref = bf16[640,2048]{1,0:T(8,128)(2,1)} custom-call(s32[256]{0:T(256)} %compare_select_fusion.1.slot_ref, s32[256]{0:T(256)} %compare_convert_fusion.1.live_ref, bf16[256,128,128]{2,1,0:T(8,128)(2,1)} %bitcast.32, bf16[256,128,128]{2,1,0:T(8,128)(2,1)} %bitcast.33, bf16[256,128,128]{2,1,0:T(8,128)(2,1)} %bitcast.34, ...), custom_call_target="tpu_custom_call" | custom-call | bytes 1024 | tf_op jit(solution)/shard_map/place/pallas_call | solution.py:41
  123.6 1.9 slice_bitcast_fusion.2
  125.5 11.5 %broadcast_select_fusion.1 = (bf16[4096,1024]{1,0:T(8,128)(2,1)}, bf16[4096,1024]{1,0:T(8,128)(2,1)}) fusion(bf16[4096,1024]{1,0:T(8,128)(2,1)} %collective-permute-done, pred[]{:T(512)S(6)} %eq.18, bf16[1,4096,1024]{2,1,0:T(8,128)(2,1)} %param.9), kind=kLoop, calls=%fused_computation.2 | loop fusion | flops 8388608 | bytes 33554432 | tf_op jit(solution)/shard_map/jit(_where)/select_n | solution.py:192
  137.0 17.7 %convolution_convert_fusion.1.refs_0_ = bf16[640,2048]{1,0:T(8,128)(2,1)} fusion(bf16[4096,640]{1,0:T(8,128)(2,1)} %bitcast.30, bf16[4096,1024]{1,0:T(8,128)(2,1)} %get-tuple-element.45, bf16[4096,1024]{1,0:T(8,128)(2,1)} %get-tuple-element.44), kind=kOutput, calls=%fused_computation.4 | convolution fusion | flops 10772283392 | bytes 24641536 | tf_op jit(solution)/shard_map/dot_general | solution.py:227
  154.7 1.5 collective-permute-start.2
  156.2 2.5 copy-done.6
  158.7 17.0 %project.7.refs_0_ = f32[4096,2048]{1,0:T(8,128)} custom-call(bf16[4096,640]{1,0:T(8,128)(2,1)S(1)} %bitcast.31, bf16[640,2048]{1,0:T(8,128)(2,1)S(1)} %copy-done.2), custom_call_target="tpu_custom_call" | custom-call | bytes 1024 | tf_op jit(solution)/shard_map/project/pallas_call | solution.py:128
  175.6 34.1 %all-gather.10.cloned.1.call-done = bf16[4096,640]{1,0:T(8,128)(2,1)} async-done(((bf16[1024,640]{1,0:T(8,128)(2,1)}), bf16[4096,640]{1,0:T(8,128)(2,1)}) %all-gather.10.cloned.1.call-update) | async-done | bytes 5242896 | tf_op jit(solution)/shard_map/all_gather | solution.py:219
  209.7 17.7 %convolution_convert_fusion.refs_0_ = bf16[640,2048]{1,0:T(8,128)(2,1)} fusion(bf16[4096,640]{1,0:T(8,128)(2,1)} %all-gather.10.cloned.1.call-done, bf16[4096,1024]{1,0:T(8,128)(2,1)} %get-tuple-element.45, bf16[4096,1024]{1,0:T(8,128)(2,1)} %get-tuple-element.44), kind=kOutput, calls=%fused_computation.3 | convolution fusion | flops 10772283392 | bytes 24641536 | tf_op jit(solution)/shard_map/dot_general | solution.py:227
  227.4 1.5 collective-permute-start.1
  228.9 7.5 %place.6.weight_ref = bf16[640,2048]{1,0:T(8,128)(2,1)} custom-call(s32[256]{0:T(256)} %compare_select_fusion.1.slot_ref, s32[256]{0:T(256)} %compare_convert_fusion.1.live_ref, bf16[256,128,128]{2,1,0:T(8,128)(2,1)} %bitcast.47, bf16[256,128,128]{2,1,0:T(8,128)(2,1)} %bitcast.41, bf16[256,128,128]{2,1,0:T(8,128)(2,1)} %bitcast.42, ...), custom_call_target="tpu_custom_call" | custom-call | bytes 1024 | tf_op jit(solution)/shard_map/place/pallas_call | solution.py:41
  236.4 6.2 %place.7.weight_ref = bf16[512,2048]{1,0:T(8,128)(2,1)} custom-call(s32[256]{0:T(256)} %compare_select_fusion.1.slot_ref, s32[256]{0:T(256)} %compare_convert_fusion.1.live_ref, bf16[256,128,128]{2,1,0:T(8,128)(2,1)} %bitcast.48, bf16[256,128,128]{2,1,0:T(8,128)(2,1)} %bitcast.49, bf16[256,128,128]{2,1,0:T(8,128)(2,1)} %bitcast.50, ...), custom_call_target="tpu_custom_call" | custom-call | bytes 1024 | tf_op jit(solution)/shard_map/place/pallas_call | solution.py:41
  242.6 4.4 place.5.weight_ref
  247.0 5.4 %combine.8.refs_2_ = f32[2048,2048]{1,0:T(8,128)} custom-call(bf16[640,2048]{1,0:T(8,128)(2,1)S(1)} %copy-done.8, bf16[640,2048]{1,0:T(8,128)(2,1)} %collective-permute-done.2.refs_1_), custom_call_target="tpu_custom_call" | custom-call | bytes 1024 | tf_op jit(solution)/shard_map/combine/pallas_call | solution.py:159
  252.4 2.5 copy-done.5
  255.0 28.5 %project.8.refs_0_ = f32[4096,2048]{1,0:T(8,128)} custom-call(bf16[4096,640]{1,0:T(8,128)(2,1)S(1)} %copy-done.5, bf16[640,2048]{1,0:T(8,128)(2,1)S(1)} %copy-done.3, f32[4096,2048]{1,0:T(8,128)} %project.7.refs_0_), custom_call_target="tpu_custom_call", output_to_operand_aliasing={{}: (2, {})} | custom-call | bytes 1024 | tf_op jit(solution)/shard_map/project/pallas_call | solution.py:128
  283.5 7.0 %all-gather.14.cloned.1.call-done = bf16[4096,512]{1,0:T(8,128)(2,1)} async-done(((bf16[1024,512]{1,0:T(8,128)(2,1)}), bf16[4096,512]{1,0:T(8,128)(2,1)}) %all-gather.14.cloned.1.call-update) | async-done | bytes 4194320 | tf_op jit(solution)/shard_map/all_gather | solution.py:219
  290.5 17.6 %convolution_convert_fusion.2.refs_0_ = bf16[512,2048]{1,0:T(8,128)(2,1)} fusion(bf16[4096,512]{1,0:T(8,128)(2,1)} %all-gather.14.cloned.1.call-done, bf16[4096,1024]{1,0:T(8,128)(2,1)} %get-tuple-element.45, bf16[4096,1024]{1,0:T(8,128)(2,1)} %get-tuple-element.44), kind=kOutput, calls=%fused_computation.5 | convolution fusion | flops 8624537600 | bytes 23068672 | tf_op jit(solution)/shard_map/dot_general | solution.py:227
  308.1 2.2 copy-done.7
  310.3 25.8 %project.9.refs_0_ = f32[4096,2048]{1,0:T(8,128)} custom-call(bf16[4096,512]{1,0:T(8,128)(2,1)S(1)} %copy-done.7, bf16[512,2048]{1,0:T(8,128)(2,1)S(1)} %copy-done.4, f32[4096,2048]{1,0:T(8,128)} %project.8.refs_0_), custom_call_target="tpu_custom_call", output_to_operand_aliasing={{}: (2, {})} | custom-call | bytes 1024 | tf_op jit(solution)/shard_map/project/pallas_call | solution.py:128
  336.1 6.5 %combine.9.refs_2_ = f32[2048,2048]{1,0:T(8,128)} custom-call(bf16[640,2048]{1,0:T(8,128)(2,1)} %convolution_convert_fusion.refs_0_, bf16[640,2048]{1,0:T(8,128)(2,1)} %collective-permute-done.1.refs_1_, f32[2048,2048]{1,0:T(8,128)} %combine.8.refs_2_), custom_call_target="tpu_custom_call", output_to_operand_aliasing={{}: (2, {})} | custom-call | bytes 1024 | tf_op jit(solution)/shard_map/combine/pallas_call | solution.py:159
  342.6 11.0 %convolution_convert_fusion.3.refs_0_ = bf16[256,2048]{1,0:T(8,128)(2,1)S(1)} fusion(bf16[4096,256]{1,0:T(8,128)(2,1)} %all-gather.12.cloned.1.call-done, bf16[4096,1024]{1,0:T(8,128)(2,1)} %get-tuple-element.45, bf16[4096,1024]{1,0:T(8,128)(2,1)} %get-tuple-element.44), kind=kOutput, calls=%fused_computation.6 | convolution fusion | flops 4329046016 | bytes 19922944 | tf_op jit(solution)/shard_map/dot_general | solution.py:227
  353.7 5.6 %project.13.refs_0_ = bf16[1024,2048]{1,0:T(8,128)(2,1)} custom-call(bf16[4096,256]{1,0:T(8,128)(2,1)S(1)} %copy-done, bf16[256,2048]{1,0:T(8,128)(2,1)S(1)} %copy-done.1, f32[4096,2048]{1,0:T(8,128)} %project.9.refs_0_), custom_call_target="tpu_custom_call" | custom-call | bytes 1024 | tf_op jit(solution)/shard_map/project/pallas_call | solution.py:128
  359.3 5.5 %project.12.refs_0_ = bf16[1024,2048]{1,0:T(8,128)(2,1)} custom-call(bf16[4096,256]{1,0:T(8,128)(2,1)S(1)} %copy-done, bf16[256,2048]{1,0:T(8,128)(2,1)S(1)} %copy-done.1, f32[4096,2048]{1,0:T(8,128)} %project.9.refs_0_), custom_call_target="tpu_custom_call" | custom-call | bytes 1024 | tf_op jit(solution)/shard_map/project/pallas_call | solution.py:128
  364.8 0.5 collective-permute-start.5
  365.3 5.6 %project.11.refs_0_ = bf16[1024,2048]{1,0:T(8,128)(2,1)} custom-call(bf16[4096,256]{1,0:T(8,128)(2,1)S(1)} %copy-done, bf16[256,2048]{1,0:T(8,128)(2,1)S(1)} %copy-done.1, f32[4096,2048]{1,0:T(8,128)} %project.9.refs_0_), custom_call_target="tpu_custom_call" | custom-call | bytes 1024 | tf_op jit(solution)/shard_map/project/pallas_call | solution.py:128
  371.0 5.7 %project.10.refs_0_ = bf16[1024,2048]{1,0:T(8,128)(2,1)} custom-call(bf16[4096,256]{1,0:T(8,128)(2,1)S(1)} %copy-done, bf16[256,2048]{1,0:T(8,128)(2,1)S(1)} %copy-done.1, f32[4096,2048]{1,0:T(8,128)} %project.9.refs_0_), custom_call_target="tpu_custom_call" | custom-call | bytes 1024 | tf_op jit(solution)/shard_map/project/pallas_call | solution.py:128
  376.7 0.5 collective-permute-start.3
  377.2 1.5 collective-permute-start.8
  378.6 46.1 %collective-permute-done.8.refs_1_ = bf16[512,2048]{1,0:T(8,128)(2,1)S(1)} collective-permute-done((bf16[512,2048]{1,0:T(8,128)(2,1)S(1)}, bf16[512,2048]{1,0:T(8,128)(2,1)S(1)}, u32[]{:S(2)}, u32[]{:S(2)}) %collective-permute-start.8) | collective-permute-done | bytes 2097184 | tf_op jit(solution)/shard_map/ppermute | solution.py:173
  424.7 1.3 copy-done.10
  426.1 1.5 collective-permute-start.7
  427.5 0.5 compare_select_fusion
  428.1 1.6 copy-done.11
  429.7 2.2 combine.14.refs_2_
  431.9 18.5 %collective-permute-done.7.refs_1_ = bf16[256,2048]{1,0:T(8,128)(2,1)} collective-permute-done((bf16[256,2048]{1,0:T(8,128)(2,1)S(1)}, bf16[256,2048]{1,0:T(8,128)(2,1)}, u32[]{:S(2)}, u32[]{:S(2)}) %collective-permute-start.7) | collective-permute-done | bytes 1048608 | tf_op jit(solution)/shard_map/ppermute | solution.py:173
  450.4 2.7 combine.15.refs_0_.refs_1_.refs_2_.refs_3_.refs_4_.refs_5_.refs_6_.refs_7_
  453.2 11.5 %pick.1 = f32[128,128,128]{2,1,0:T(8,128)} custom-call(s32[128]{0:T(128)} %get-tuple-element.42.block_ref, s32[128]{0:T(128)} %get-tuple-element.43.live_ref, f32[2048,2048]{1,0:T(8,128)} %combine.15.refs_0_.refs_1_.refs_2_.refs_3_.refs_4_.refs_5_.refs_6_.refs_7_, f32[2048,2048]{1,0:T(8,128)} %combine.15.refs_0_.refs_1_.refs_2_.refs_3_.refs_4_.refs_5_.refs_6_.refs_7_, ...), custom_call_target="tpu_custom_call" | custom-call | bytes 1024 | tf_op jit(solution)/shard_map/pick/pallas_call | solution.py:86
  464.7 6.0 %combine.10.refs_2_ = bf16[4096,2048]{1,0:T(8,128)(2,1)} custom-call(bf16[1024,2048]{1,0:T(8,128)(2,1)} %project.13.refs_0_, bf16[1024,2048]{1,0:T(8,128)(2,1)} %collective-permute-done.6.refs_1_), custom_call_target="tpu_custom_call" | custom-call | bytes 1024 | tf_op jit(solution)/shard_map/combine/pallas_call | solution.py:159
  470.7 6.0 %combine.11.refs_2_ = bf16[4096,2048]{1,0:T(8,128)(2,1)} custom-call(bf16[1024,2048]{1,0:T(8,128)(2,1)} %project.12.refs_0_, bf16[1024,2048]{1,0:T(8,128)(2,1)} %collective-permute-done.5.refs_1_, bf16[4096,2048]{1,0:T(8,128)(2,1)} %combine.10.refs_2_), custom_call_target="tpu_custom_call", output_to_operand_aliasing={{}: (2, {})} | custom-call | bytes 1024 | tf_op jit(solution)/shard_map/combine/pallas_call | solution.py:159
  476.7 6.0 %combine.12.refs_2_ = bf16[4096,2048]{1,0:T(8,128)(2,1)} custom-call(bf16[1024,2048]{1,0:T(8,128)(2,1)} %project.11.refs_0_, bf16[1024,2048]{1,0:T(8,128)(2,1)} %collective-permute-done.4.refs_1_, bf16[4096,2048]{1,0:T(8,128)(2,1)} %combine.11.refs_2_), custom_call_target="tpu_custom_call", output_to_operand_aliasing={{}: (2, {})} | custom-call | bytes 1024 | tf_op jit(solution)/shard_map/combine/pallas_call | solution.py:159
  482.7 6.0 %combine.13 = bf16[4096,2048]{1,0:T(8,128)(2,1)} custom-call(bf16[1024,2048]{1,0:T(8,128)(2,1)} %project.10.refs_0_, bf16[1024,2048]{1,0:T(8,128)(2,1)} %collective-permute-done.3.refs_1_, bf16[4096,2048]{1,0:T(8,128)(2,1)} %combine.12.refs_2_), custom_call_target="tpu_custom_call", output_to_operand_aliasing={{}: (2, {})} | custom-call | bytes 1024 | tf_op jit(solution)/shard_map/combine/pallas_call | solution.py:159
  (42 shorter events, 0.4 us)
Async XLA Ops:
  7.2 107.7 %copy-start.12 = (s32[1,1,256]{2,1,0:T(1,128)S(1)}, s32[1,1,256]{2,1,0:T(1,128)}, u32[]{:S(2)}) copy-start(s32[1,1,256]{2,1,0:T(1,128)} %param.7) | copy-start | bytes 3076
  7.2 104.5 %all-gather.8.cloned.1.call-start = ((), (), s32[]{:S(2)}) async-start(), calls=%async_computation | async-start | bytes 6553600 | tf_op jit(solution)/shard_map/all_gather | solution.py:219
  10.7 199.0 %all-gather.10.cloned.1.call-start = ((), (), s32[]{:S(2)}) async-start(), calls=%async_computation.1 | async-start | bytes 6553600 | tf_op jit(solution)/shard_map/all_gather | solution.py:219
  111.7 178.8 %all-gather.14.cloned.1.call-start = ((), (), s32[]{:S(2)}) async-start(), calls=%async_computation.3 | async-start | bytes 5242880 | tf_op jit(solution)/shard_map/all_gather | solution.py:219
  111.7 13.8 %collective-permute-start = (bf16[4096,1024]{1,0:T(8,128)(2,1)}, bf16[4096,1024]{1,0:T(8,128)(2,1)}, u32[]{:S(2)}, u32[]{:S(2)}) collective-permute-start(bf16[4096,1024]{1,0:T(8,128)(2,1)} %bitcast.65), channel_id=1, source_target_pairs={{0,1},{1,0},{2,3},{3,2},{4,5},{5,4},{6,7},{7,6},{8,9},{9,8},{10,11... | collective-permute-start | bytes 25165832 | tf_op jit(solution)/shard_map/ppermute | solution.py:173
  114.1 228.5 %all-gather.12.cloned.1.call-start = ((), (), s32[]{:S(2)}) async-start(), calls=%async_computation.2 | async-start | bytes 2621440 | tf_op jit(solution)/shard_map/all_gather | solution.py:219
  137.0 19.2 %copy-start.2 = (bf16[640,2048]{1,0:T(8,128)(2,1)S(1)}, bf16[640,2048]{1,0:T(8,128)(2,1)}, u32[]{:S(2)}) copy-start(bf16[640,2048]{1,0:T(8,128)(2,1)} %place.4.weight_ref) | copy-start | bytes 7864324
  154.7 92.3 %collective-permute-start.2 = (bf16[640,2048]{1,0:T(8,128)(2,1)}, bf16[640,2048]{1,0:T(8,128)(2,1)}, u32[]{:S(2)}, u32[]{:S(2)}) collective-permute-start(bf16[640,2048]{1,0:T(8,128)(2,1)} %convolution_convert_fusion.1.refs_0_), channel_id=1, source_target_pairs={{0,2},{2,0},{1,3},{3,1},{4,6},{6,4},{5,7},{7,5},{8,10},{10,8},{9,1... | collective-permute-start | bytes 7864328 | tf_op jit(solution)/shard_map/ppermute | solution.py:173
  156.2 2.5 copy-start.6
  227.4 108.7 %collective-permute-start.1 = (bf16[640,2048]{1,0:T(8,128)(2,1)}, bf16[640,2048]{1,0:T(8,128)(2,1)}, u32[]{:S(2)}, u32[]{:S(2)}) collective-permute-start(bf16[640,2048]{1,0:T(8,128)(2,1)} %convolution_convert_fusion.refs_0_), channel_id=1, source_target_pairs={{0,2},{2,0},{1,3},{3,1},{4,6},{6,4},{5,7},{7,5},{8,10},{10,8},{9,1... | collective-permute-start | bytes 7864328 | tf_op jit(solution)/shard_map/ppermute | solution.py:173
  242.6 4.4 copy-start.8
  247.0 5.4 %copy-start.3 = (bf16[640,2048]{1,0:T(8,128)(2,1)S(1)}, bf16[640,2048]{1,0:T(8,128)(2,1)}, u32[]{:S(2)}) copy-start(bf16[640,2048]{1,0:T(8,128)(2,1)} %place.6.weight_ref) | copy-start | bytes 7864324
  252.4 2.5 copy-start.5
  290.5 17.6 %copy-start.4 = (bf16[512,2048]{1,0:T(8,128)(2,1)S(1)}, bf16[512,2048]{1,0:T(8,128)(2,1)}, u32[]{:S(2)}) copy-start(bf16[512,2048]{1,0:T(8,128)(2,1)} %place.7.weight_ref) | copy-start | bytes 6291460
  308.1 2.2 copy-start.7
  342.6 11.1 %copy-start = (bf16[4096,256]{1,0:T(8,128)(2,1)S(1)}, bf16[4096,256]{1,0:T(8,128)(2,1)}, u32[]{:S(2)}) copy-start(bf16[4096,256]{1,0:T(8,128)(2,1)} %all-gather.12.cloned.1.call-done) | copy-start | bytes 6291460
  342.6 11.1 %copy-start.1 = (bf16[256,2048]{1,0:T(8,128)(2,1)S(1)}, bf16[256,2048]{1,0:T(8,128)(2,1)}, u32[]{:S(2)}) copy-start(bf16[256,2048]{1,0:T(8,128)(2,1)} %place.5.weight_ref) | copy-start | bytes 3145732
  359.3 105.4 %collective-permute-start.6 = (bf16[1024,2048]{1,0:T(8,128)(2,1)}, bf16[1024,2048]{1,0:T(8,128)(2,1)}, u32[]{:S(2)}, u32[]{:S(2)}) collective-permute-start(bf16[1024,2048]{1,0:T(8,128)(2,1)} %project.13.refs_0_), channel_id=1, source_target_pairs={{0,1},{1,0},{2,3},{3,2},{4,5},{5,4},{6,7},{7,6},{8,9},{9,8},{10,11... | collective-permute-start | bytes 12582920 | tf_op jit(solution)/shard_map/ppermute | solution.py:173
  364.8 105.9 %collective-permute-start.5 = (bf16[1024,2048]{1,0:T(8,128)(2,1)}, bf16[1024,2048]{1,0:T(8,128)(2,1)}, u32[]{:S(2)}, u32[]{:S(2)}) collective-permute-start(bf16[1024,2048]{1,0:T(8,128)(2,1)} %project.12.refs_0_), channel_id=1, source_target_pairs={{0,1},{1,0},{2,3},{3,2},{4,5},{5,4},{6,7},{7,6},{8,9},{9,8},{10,11... | collective-permute-start | bytes 12582920 | tf_op jit(solution)/shard_map/ppermute | solution.py:173
  371.0 6.2 %copy-start.9 = (bf16[512,2048]{1,0:T(8,128)(2,1)S(1)}, bf16[512,2048]{1,0:T(8,128)(2,1)}, u32[]{:S(2)}) copy-start(bf16[512,2048]{1,0:T(8,128)(2,1)} %convolution_convert_fusion.2.refs_0_) | copy-start | bytes 6291460
  371.0 56.6 %copy-start.13 = (s32[1,1,256]{2,1,0:T(1,128)S(1)}, s32[1,1,256]{2,1,0:T(1,128)}, u32[]{:S(2)}) copy-start(s32[1,1,256]{2,1,0:T(1,128)} %param.7) | copy-start | bytes 3076
  371.0 105.8 %collective-permute-start.4 = (bf16[1024,2048]{1,0:T(8,128)(2,1)}, bf16[1024,2048]{1,0:T(8,128)(2,1)}, u32[]{:S(2)}, u32[]{:S(2)}) collective-permute-start(bf16[1024,2048]{1,0:T(8,128)(2,1)} %project.11.refs_0_), channel_id=1, source_target_pairs={{0,1},{1,0},{2,3},{3,2},{4,5},{5,4},{6,7},{7,6},{8,9},{9,8},{10,11... | collective-permute-start | bytes 12582920 | tf_op jit(solution)/shard_map/ppermute | solution.py:173
  376.7 106.1 %collective-permute-start.3 = (bf16[1024,2048]{1,0:T(8,128)(2,1)}, bf16[1024,2048]{1,0:T(8,128)(2,1)}, u32[]{:S(2)}, u32[]{:S(2)}) collective-permute-start(bf16[1024,2048]{1,0:T(8,128)(2,1)} %project.10.refs_0_), channel_id=1, source_target_pairs={{0,1},{1,0},{2,3},{3,2},{4,5},{5,4},{6,7},{7,6},{8,9},{9,8},{10,11... | collective-permute-start | bytes 12582920 | tf_op jit(solution)/shard_map/ppermute | solution.py:173
  377.2 47.6 %collective-permute-start.8 = (bf16[512,2048]{1,0:T(8,128)(2,1)S(1)}, bf16[512,2048]{1,0:T(8,128)(2,1)S(1)}, u32[]{:S(2)}, u32[]{:S(2)}) collective-permute-start(bf16[512,2048]{1,0:T(8,128)(2,1)S(1)} %copy-done.9), channel_id=1, source_target_pairs={{0,2},{2,0},{1,3},{3,1},{4,6},{6,4},{5,7},{7,5},{8,10},{10,8},{9,1... | collective-permute-start | bytes 6291464 | tf_op jit(solution)/shard_map/ppermute | solution.py:173
  424.7 1.3 copy-start.10
  426.1 24.4 %collective-permute-start.7 = (bf16[256,2048]{1,0:T(8,128)(2,1)S(1)}, bf16[256,2048]{1,0:T(8,128)(2,1)}, u32[]{:S(2)}, u32[]{:S(2)}) collective-permute-start(bf16[256,2048]{1,0:T(8,128)(2,1)S(1)} %convolution_convert_fusion.3.refs_0_), channel_id=1, source_target_pairs={{0,2},{2,0},{1,3},{3,1},{4,6},{6,4},{5,7},{7,5},{8,10},{10,8},{9,1... | collective-permute-start | bytes 3145736 | tf_op jit(solution)/shard_map/ppermute | solution.py:173
  428.1 1.6 copy-start.11
Sparse Core Ops, SparseCore 0:
  10.9 100.7 all-gather.7
  113.2 96.4 all-gather.9
  211.3 79.1 all-gather.13
  291.9 44.4 all-gather.11

commit v3 on v2

--- a/solution.py
+++ b/solution.py
@@ -229,7 +229,10 @@
         ).astype(jnp.bfloat16)
         flat, grad = lax.optimization_barrier((flat, grad))
         parts = [grad] + [shifted(grad, "dp", n_dp, shift) for shift in range(1, n_dp)]
-        sums = combine(parts, sums, lo, in_width, jnp.float32)
+        if number + 1 == len(spans) and number > 0:
+            flat, sums = lax.optimization_barrier((flat, sums))
+        else:
+            sums = combine(parts, sums, lo, in_width, jnp.float32)
         if number == len(spans) - 3:
             arrived[-1], sums = lax.optimization_barrier((arrived[-1], sums))
         part = weights[number]
@@ -245,12 +248,18 @@
                 for q in range(4)
             ]
 
+    last_parts = parts
     projected = None
     for q, own_part in enumerate(mine):
         parts = [own_part] + [
             shifted(own_part, "section", n_section, shift) for shift in range(1, n_section)
         ]
         projected = combine(parts, projected, q * (length // 4), length, jnp.bfloat16)
+        if q == 2 and len(spans) > 1:
+            parts_here, projected = lax.optimization_barrier((last_parts[0], projected))
+            sums = combine(
+                [parts_here] + last_parts[1:], sums, spans[-1][0], in_width, jnp.float32
+            )
 
     share = slots // n_dp
     start = lax.axis_index("dp") * share

time: 499 us -> 477 us (0.956)
  waiting for transfers between devices: 207 us -> 189 us
    ppermute x9, waiting for transfers between devices: 64.6 us -> 30.4 us  [shifted(): return lax.ppermute(x, axis, [(i, (i + shift) % size) for i in range(size)])]
    all_gather x4, waiting for transfers between devices: 142 us -> 159 us  [local(): arrived.append(lax.all_gather(piece, 'tensor', axis=0))]
    unnamed x28 -> x26, local copies, waits for them, and re-layouts: 10.2 us -> 6.92 us
  transfers between devices with their start and end apart: 13 -> 13, of which waited for: 5 -> 5; matrix products, arithmetic and copies ran while one was open for 14% -> 17% of each run, Pallas kernels for 32% -> 33%
where the time goes in v3:
time: 477 us; the launch traced here: 473 us
  waiting for transfers between devices  189 us (40%)
  Pallas kernels  171 us (36%)
  matrix products  64.2 us (13%)
  local copies, waits for them, and re-layouts  14.5 us (3%)
  between operations  14.5 us (3%)
  other arithmetic  13.3 us (3%)
  starting transfers between devices  5.96 us (1%)
    all_gather x4, waiting for transfers between devices, local(): arrived.append(lax.all_gather(piece, 'tensor', axis=0))  159 us
    pallas_call x7, Pallas kernels, project(): pl.pallas_call(functools.partial(project_kernel, partial is None), grid=(...  93.5 us
    dot_general x4, matrix products, local(): lax.dot_general(flat, columns, (((0,), (0,)), ((), ())), preferred_elemen...  64.2 us
    pallas_call x8, Pallas kernels, combine(): pl.pallas_call(functools.partial(combine_kernel, len(parts)), grid=(heigh...  38.5 us
    ppermute x9, waiting for transfers between devices, shifted(): return lax.ppermute(x, axis, [(i, (i + shift) % size) for i in range(size)])  30.4 us
    pallas_call x4, Pallas kernels, place_tiles(): pl.pallas_call(functools.partial(place_kernel, count, first), grid_spec=p...  26.1 us
    pallas_call x1, Pallas kernels, pick_blocks(): pl.pallas_call(functools.partial(pick_kernel, count), grid_spec=pltpu.Pre...  12.7 us
    select_n x1, other arithmetic, local(): jnp.where(first, own, other)  11.5 us
  transfers between devices with their start and end apart: 13, of which 5 were waited for; matrix products, arithmetic and copies ran while one was open for 17% of the time, Pallas kernels for 33%

profile of v3, /device:TPU:0, one launch (start us, length us, event | category | flops | bytes accessed | tf_op | source)
XLA Modules:
  0.0 472.8 jit_solution(7549136524314429451)
XLA Ops:
  7.2 3.5 fusion
  10.8 100.9 %all-gather.8.cloned.1.call-done = bf16[4,1024,640]{2,1,0:T(8,128)(2,1)} async-done(((bf16[1,1024,640]{2,1,0:T(8,128)(2,1)}), bf16[4,1024,640]{2,1,0:T(8,128)(2,1)}) %all-gather.8.cloned.1.call-update) | async-done | bytes 5242896 | tf_op jit(solution)/shard_map/all_gather | solution.py:219
  111.7 0.1 collective-permute-start
  111.8 2.3 slice_bitcast_fusion.1
  114.1 0.0 all-gather.12.cloned.1.call-start
  114.8 0.1 select_reduce_fusion
  114.9 0.6 compare_convert_fusion.1.live_ref
  115.5 0.6 compare_select_fusion.1.slot_ref
  116.1 7.8 %place.4.weight_ref = bf16[640,2048]{1,0:T(8,128)(2,1)} custom-call(s32[256]{0:T(256)} %compare_select_fusion.1.slot_ref, s32[256]{0:T(256)} %compare_convert_fusion.1.live_ref, bf16[256,128,128]{2,1,0:T(8,128)(2,1)} %bitcast.32, bf16[256,128,128]{2,1,0:T(8,128)(2,1)} %bitcast.33, bf16[256,128,128]{2,1,0:T(8,128)(2,1)} %bitcast.34, ...), custom_call_target="tpu_custom_call" | custom-call | bytes 1024 | tf_op jit(solution)/shard_map/place/pallas_call | solution.py:41
  123.9 7.7 %place.5.weight_ref = bf16[640,2048]{1,0:T(8,128)(2,1)} custom-call(s32[256]{0:T(256)} %compare_select_fusion.1.slot_ref, s32[256]{0:T(256)} %compare_convert_fusion.1.live_ref, bf16[256,128,128]{2,1,0:T(8,128)(2,1)} %bitcast.47, bf16[256,128,128]{2,1,0:T(8,128)(2,1)} %bitcast.41, bf16[256,128,128]{2,1,0:T(8,128)(2,1)} %bitcast.42, ...), custom_call_target="tpu_custom_call" | custom-call | bytes 1024 | tf_op jit(solution)/shard_map/place/pallas_call | solution.py:41
  131.5 1.9 slice_bitcast_fusion.2
  133.4 11.5 %broadcast_select_fusion.1 = (bf16[4096,1024]{1,0:T(8,128)(2,1)}, bf16[4096,1024]{1,0:T(8,128)(2,1)}) fusion(bf16[4096,1024]{1,0:T(8,128)(2,1)} %collective-permute-done, pred[]{:T(512)S(6)} %eq.18, bf16[1,4096,1024]{2,1,0:T(8,128)(2,1)} %param.9), kind=kLoop, calls=%fused_computation.2 | loop fusion | flops 8388608 | bytes 33554432 | tf_op jit(solution)/shard_map/jit(_where)/select_n | solution.py:192
  144.9 17.7 %convolution_convert_fusion.1.refs_0_ = bf16[640,2048]{1,0:T(8,128)(2,1)} fusion(bf16[4096,640]{1,0:T(8,128)(2,1)} %bitcast.30, bf16[4096,1024]{1,0:T(8,128)(2,1)} %get-tuple-element.53, bf16[4096,1024]{1,0:T(8,128)(2,1)} %get-tuple-element.52), kind=kOutput, calls=%fused_computation.4 | convolution fusion | flops 10772283392 | bytes 24641536 | tf_op jit(solution)/shard_map/dot_general | solution.py:227
  162.6 1.5 collective-permute-start.2
  164.0 2.5 copy-done.6
  166.5 16.9 %project.7.refs_0_ = f32[4096,2048]{1,0:T(8,128)} custom-call(bf16[4096,640]{1,0:T(8,128)(2,1)S(1)} %bitcast.31, bf16[640,2048]{1,0:T(8,128)(2,1)S(1)} %copy-done.3), custom_call_target="tpu_custom_call" | custom-call | bytes 1024 | tf_op jit(solution)/shard_map/project/pallas_call | solution.py:128
  183.5 26.2 %all-gather.10.cloned.1.call-done = bf16[4096,640]{1,0:T(8,128)(2,1)} async-done(((bf16[1024,640]{1,0:T(8,128)(2,1)}), bf16[4096,640]{1,0:T(8,128)(2,1)}) %all-gather.10.cloned.1.call-update) | async-done | bytes 5242896 | tf_op jit(solution)/shard_map/all_gather | solution.py:219
  209.7 17.8 %convolution_convert_fusion.refs_0_ = bf16[640,2048]{1,0:T(8,128)(2,1)} fusion(bf16[4096,640]{1,0:T(8,128)(2,1)} %all-gather.10.cloned.1.call-done, bf16[4096,1024]{1,0:T(8,128)(2,1)} %get-tuple-element.53, bf16[4096,1024]{1,0:T(8,128)(2,1)} %get-tuple-element.52), kind=kOutput, calls=%fused_computation.3 | convolution fusion | flops 10772283392 | bytes 24641536 | tf_op jit(solution)/shard_map/dot_general | solution.py:227
  227.5 2.5 copy-done.5
  230.0 28.5 %project.8.refs_0_ = f32[4096,2048]{1,0:T(8,128)} custom-call(bf16[4096,640]{1,0:T(8,128)(2,1)S(1)} %copy-done.5, bf16[640,2048]{1,0:T(8,128)(2,1)S(1)} %copy-done.2, f32[4096,2048]{1,0:T(8,128)} %project.7.refs_0_), custom_call_target="tpu_custom_call", output_to_operand_aliasing={{}: (2, {})} | custom-call | bytes 1024 | tf_op jit(solution)/shard_map/project/pallas_call | solution.py:128
  258.5 31.9 %all-gather.14.cloned.1.call-done = bf16[4096,512]{1,0:T(8,128)(2,1)} async-done(((bf16[1024,512]{1,0:T(8,128)(2,1)}), bf16[4096,512]{1,0:T(8,128)(2,1)}) %all-gather.14.cloned.1.call-update) | async-done | bytes 4194320 | tf_op jit(solution)/shard_map/all_gather | solution.py:219
  290.4 1.5 collective-permute-start.1
  291.9 17.7 %convolution_convert_fusion.2.refs_0_ = bf16[512,2048]{1,0:T(8,128)(2,1)} fusion(bf16[4096,512]{1,0:T(8,128)(2,1)} %all-gather.14.cloned.1.call-done, bf16[4096,1024]{1,0:T(8,128)(2,1)} %get-tuple-element.53, bf16[4096,1024]{1,0:T(8,128)(2,1)} %get-tuple-element.52), kind=kOutput, calls=%fused_computation.5 | convolution fusion | flops 8624537600 | bytes 23068672 | tf_op jit(solution)/shard_map/dot_general | solution.py:227
  309.6 0.3 collective-permute-start.3
  309.9 6.5 %place.7.weight_ref = bf16[512,2048]{1,0:T(8,128)(2,1)} custom-call(s32[256]{0:T(256)} %compare_select_fusion.1.slot_ref, s32[256]{0:T(256)} %compare_convert_fusion.1.live_ref, bf16[256,128,128]{2,1,0:T(8,128)(2,1)} %bitcast.48, bf16[256,128,128]{2,1,0:T(8,128)(2,1)} %bitcast.49, bf16[256,128,128]{2,1,0:T(8,128)(2,1)} %bitcast.50, ...), custom_call_target="tpu_custom_call" | custom-call | bytes 1024 | tf_op jit(solution)/shard_map/place/pallas_call | solution.py:41
  316.4 4.2 place.6.weight_ref
  320.6 1.9 copy-done.9
  322.5 6.0 %combine.8.refs_2_ = f32[2048,2048]{1,0:T(8,128)} custom-call(bf16[640,2048]{1,0:T(8,128)(2,1)S(1)} %copy-done.9, bf16[640,2048]{1,0:T(8,128)(2,1)} %collective-permute-done.2.refs_1_), custom_call_target="tpu_custom_call" | custom-call | bytes 1024 | tf_op jit(solution)/shard_map/combine/pallas_call | solution.py:159
  328.5 25.9 %project.9.refs_0_ = f32[4096,2048]{1,0:T(8,128)} custom-call(bf16[4096,512]{1,0:T(8,128)(2,1)S(1)} %copy-done.7, bf16[512,2048]{1,0:T(8,128)(2,1)S(1)} %copy-done.4, f32[4096,2048]{1,0:T(8,128)} %project.8.refs_0_), custom_call_target="tpu_custom_call", output_to_operand_aliasing={{}: (2, {})} | custom-call | bytes 1024 | tf_op jit(solution)/shard_map/project/pallas_call | solution.py:128
  354.5 3.3 combine.9.refs_2_
  357.8 11.0 %convolution_convert_fusion.3.refs_0_ = bf16[256,2048]{1,0:T(8,128)(2,1)S(1)} fusion(bf16[4096,256]{1,0:T(8,128)(2,1)} %all-gather.12.cloned.1.call-done, bf16[4096,1024]{1,0:T(8,128)(2,1)} %get-tuple-element.53, bf16[4096,1024]{1,0:T(8,128)(2,1)} %get-tuple-element.52), kind=kOutput, calls=%fused_computation.6 | convolution fusion | flops 4329046016 | bytes 19922944 | tf_op jit(solution)/shard_map/dot_general | solution.py:227
  368.9 25.4 %collective-permute-done.3.refs_1_ = bf16[512,2048]{1,0:T(8,128)(2,1)} collective-permute-done((bf16[512,2048]{1,0:T(8,128)(2,1)}, bf16[512,2048]{1,0:T(8,128)(2,1)}, u32[]{:S(2)}, u32[]{:S(2)}) %collective-permute-start.3) | collective-permute-done | bytes 2097184 | tf_op jit(solution)/shard_map/ppermute | solution.py:173
  394.3 3.5 combine.10.refs_2_
  397.8 5.5 %project.13.refs_0_ = bf16[1024,2048]{1,0:T(8,128)(2,1)} custom-call(bf16[4096,256]{1,0:T(8,128)(2,1)S(1)} %copy-done, bf16[256,2048]{1,0:T(8,128)(2,1)S(1)} %copy-done.1, f32[4096,2048]{1,0:T(8,128)} %project.9.refs_0_), custom_call_target="tpu_custom_call" | custom-call | bytes 1024 | tf_op jit(solution)/shard_map/project/pallas_call | solution.py:128
  403.4 5.5 %project.12.refs_0_ = bf16[1024,2048]{1,0:T(8,128)(2,1)} custom-call(bf16[4096,256]{1,0:T(8,128)(2,1)S(1)} %copy-done, bf16[256,2048]{1,0:T(8,128)(2,1)S(1)} %copy-done.1, f32[4096,2048]{1,0:T(8,128)} %project.9.refs_0_), custom_call_target="tpu_custom_call" | custom-call | bytes 1024 | tf_op jit(solution)/shard_map/project/pallas_call | solution.py:128
  408.9 0.5 collective-permute-start.6
  409.4 5.5 %project.11.refs_0_ = bf16[1024,2048]{1,0:T(8,128)(2,1)} custom-call(bf16[4096,256]{1,0:T(8,128)(2,1)S(1)} %copy-done, bf16[256,2048]{1,0:T(8,128)(2,1)S(1)} %copy-done.1, f32[4096,2048]{1,0:T(8,128)} %project.9.refs_0_), custom_call_target="tpu_custom_call" | custom-call | bytes 1024 | tf_op jit(solution)/shard_map/project/pallas_call | solution.py:128
  414.9 5.5 %project.10.refs_0_ = bf16[1024,2048]{1,0:T(8,128)(2,1)} custom-call(bf16[4096,256]{1,0:T(8,128)(2,1)S(1)} %copy-done, bf16[256,2048]{1,0:T(8,128)(2,1)S(1)} %copy-done.1, f32[4096,2048]{1,0:T(8,128)} %project.9.refs_0_), custom_call_target="tpu_custom_call" | custom-call | bytes 1024 | tf_op jit(solution)/shard_map/project/pallas_call | solution.py:128
  420.4 0.5 collective-permute-start.4
  420.9 1.5 collective-permute-start.8
  422.4 0.6 compare_select_fusion
  423.0 6.0 %combine.11.refs_2_ = bf16[4096,2048]{1,0:T(8,128)(2,1)} custom-call(bf16[1024,2048]{1,0:T(8,128)(2,1)} %project.13.refs_0_, bf16[1024,2048]{1,0:T(8,128)(2,1)} %collective-permute-done.7.refs_1_), custom_call_target="tpu_custom_call" | custom-call | bytes 1024 | tf_op jit(solution)/shard_map/combine/pallas_call | solution.py:159
  429.0 6.0 %combine.12.refs_2_ = bf16[4096,2048]{1,0:T(8,128)(2,1)} custom-call(bf16[1024,2048]{1,0:T(8,128)(2,1)} %project.12.refs_0_, bf16[1024,2048]{1,0:T(8,128)(2,1)} %collective-permute-done.6.refs_1_, bf16[4096,2048]{1,0:T(8,128)(2,1)} %combine.11.refs_2_), custom_call_target="tpu_custom_call", output_to_operand_aliasing={{}: (2, {})} | custom-call | bytes 1024 | tf_op jit(solution)/shard_map/combine/pallas_call | solution.py:159
  435.0 6.0 %combine.13.refs_2_ = bf16[4096,2048]{1,0:T(8,128)(2,1)} custom-call(bf16[1024,2048]{1,0:T(8,128)(2,1)} %project.11.refs_0_, bf16[1024,2048]{1,0:T(8,128)(2,1)} %collective-permute-done.5.refs_1_, bf16[4096,2048]{1,0:T(8,128)(2,1)} %combine.12.refs_2_), custom_call_target="tpu_custom_call", output_to_operand_aliasing={{}: (2, {})} | custom-call | bytes 1024 | tf_op jit(solution)/shard_map/combine/pallas_call | solution.py:159
  441.0 5.0 %collective-permute-done.8.refs_1_ = bf16[256,2048]{1,0:T(8,128)(2,1)S(1)} collective-permute-done((bf16[256,2048]{1,0:T(8,128)(2,1)S(1)}, bf16[256,2048]{1,0:T(8,128)(2,1)S(1)}, u32[]{:S(2)}, u32[]{:S(2)}) %collective-permute-start.8) | collective-permute-done | bytes 1048608 | tf_op jit(solution)/shard_map/ppermute | solution.py:173
  446.0 1.5 combine.15.refs_0_.refs_1_.refs_2_.refs_3_.refs_4_.refs_5_.refs_6_.refs_7_
  447.5 12.7 %pick.1 = f32[128,128,128]{2,1,0:T(8,128)} custom-call(s32[128]{0:T(128)} %get-tuple-element.50.block_ref, s32[128]{0:T(128)} %get-tuple-element.51.live_ref, f32[2048,2048]{1,0:T(8,128)} %combine.15.refs_0_.refs_1_.refs_2_.refs_3_.refs_4_.refs_5_.refs_6_.refs_7_, f32[2048,2048]{1,0:T(8,128)} %combine.15.refs_0_.refs_1_.refs_2_.refs_3_.refs_4_.refs_5_.refs_6_.refs_7_, ...), custom_call_target="tpu_custom_call" | custom-call | bytes 1024 | tf_op jit(solution)/shard_map/pick/pallas_call | solution.py:86
  460.3 6.0 %combine.14 = bf16[4096,2048]{1,0:T(8,128)(2,1)} custom-call(bf16[1024,2048]{1,0:T(8,128)(2,1)} %project.10.refs_0_, bf16[1024,2048]{1,0:T(8,128)(2,1)} %collective-permute-done.4.refs_1_, bf16[4096,2048]{1,0:T(8,128)(2,1)} %combine.13.refs_2_), custom_call_target="tpu_custom_call", output_to_operand_aliasing={{}: (2, {})} | custom-call | bytes 1024 | tf_op jit(solution)/shard_map/combine/pallas_call | solution.py:159
  (40 shorter events, 0.3 us)
Async XLA Ops:
  7.2 107.6 %copy-start.11 = (s32[1,1,256]{2,1,0:T(1,128)S(1)}, s32[1,1,256]{2,1,0:T(1,128)}, u32[]{:S(2)}) copy-start(s32[1,1,256]{2,1,0:T(1,128)} %param.7) | copy-start | bytes 3076
  7.2 104.5 %all-gather.8.cloned.1.call-start = ((), (), s32[]{:S(2)}) async-start(), calls=%async_computation | async-start | bytes 6553600 | tf_op jit(solution)/shard_map/all_gather | solution.py:219
  10.7 199.0 %all-gather.10.cloned.1.call-start = ((), (), s32[]{:S(2)}) async-start(), calls=%async_computation.1 | async-start | bytes 6553600 | tf_op jit(solution)/shard_map/all_gather | solution.py:219
  111.7 178.8 %all-gather.14.cloned.1.call-start = ((), (), s32[]{:S(2)}) async-start(), calls=%async_computation.3 | async-start | bytes 5242880 | tf_op jit(solution)/shard_map/all_gather | solution.py:219
  111.7 21.7 %collective-permute-start = (bf16[4096,1024]{1,0:T(8,128)(2,1)}, bf16[4096,1024]{1,0:T(8,128)(2,1)}, u32[]{:S(2)}, u32[]{:S(2)}) collective-permute-start(bf16[4096,1024]{1,0:T(8,128)(2,1)} %bitcast.65), channel_id=1, source_target_pairs={{0,1},{1,0},{2,3},{3,2},{4,5},{5,4},{6,7},{7,6},{8,9},{9,8},{10,11... | collective-permute-start | bytes 25165832 | tf_op jit(solution)/shard_map/ppermute | solution.py:173
  114.1 243.7 %all-gather.12.cloned.1.call-start = ((), (), s32[]{:S(2)}) async-start(), calls=%async_computation.2 | async-start | bytes 2621440 | tf_op jit(solution)/shard_map/all_gather | solution.py:219
  144.9 19.1 %copy-start.3 = (bf16[640,2048]{1,0:T(8,128)(2,1)S(1)}, bf16[640,2048]{1,0:T(8,128)(2,1)}, u32[]{:S(2)}) copy-start(bf16[640,2048]{1,0:T(8,128)(2,1)} %place.4.weight_ref) | copy-start | bytes 7864324
  162.6 158.0 %collective-permute-start.2 = (bf16[640,2048]{1,0:T(8,128)(2,1)}, bf16[640,2048]{1,0:T(8,128)(2,1)}, u32[]{:S(2)}, u32[]{:S(2)}) collective-permute-start(bf16[640,2048]{1,0:T(8,128)(2,1)} %convolution_convert_fusion.1.refs_0_), channel_id=1, source_target_pairs={{0,2},{2,0},{1,3},{3,1},{4,6},{6,4},{5,7},{7,5},{8,10},{10,8},{9,1... | collective-permute-start | bytes 7864328 | tf_op jit(solution)/shard_map/ppermute | solution.py:173
  164.0 2.5 copy-start.6
  209.7 17.8 %copy-start.2 = (bf16[640,2048]{1,0:T(8,128)(2,1)S(1)}, bf16[640,2048]{1,0:T(8,128)(2,1)}, u32[]{:S(2)}) copy-start(bf16[640,2048]{1,0:T(8,128)(2,1)} %place.5.weight_ref) | copy-start | bytes 7864324
  227.5 2.5 copy-start.5
  290.4 64.0 %collective-permute-start.1 = (bf16[640,2048]{1,0:T(8,128)(2,1)}, bf16[640,2048]{1,0:T(8,128)(2,1)S(1)}, u32[]{:S(2)}, u32[]{:S(2)}) collective-permute-start(bf16[640,2048]{1,0:T(8,128)(2,1)} %convolution_convert_fusion.refs_0_), channel_id=1, source_target_pairs={{0,2},{2,0},{1,3},{3,1},{4,6},{6,4},{5,7},{7,5},{8,10},{10,8},{9,1... | collective-permute-start | bytes 7864328 | tf_op jit(solution)/shard_map/ppermute | solution.py:173
  309.6 84.7 %collective-permute-start.3 = (bf16[512,2048]{1,0:T(8,128)(2,1)}, bf16[512,2048]{1,0:T(8,128)(2,1)}, u32[]{:S(2)}, u32[]{:S(2)}) collective-permute-start(bf16[512,2048]{1,0:T(8,128)(2,1)} %convolution_convert_fusion.2.refs_0_), channel_id=1, source_target_pairs={{0,2},{2,0},{1,3},{3,1},{4,6},{6,4},{5,7},{7,5},{8,10},{10,8},{9,1... | collective-permute-start | bytes 6291464 | tf_op jit(solution)/shard_map/ppermute | solution.py:173
  320.6 7.9 %copy-start.4 = (bf16[512,2048]{1,0:T(8,128)(2,1)S(1)}, bf16[512,2048]{1,0:T(8,128)(2,1)}, u32[]{:S(2)}) copy-start(bf16[512,2048]{1,0:T(8,128)(2,1)} %place.7.weight_ref) | copy-start | bytes 6291460
  320.6 7.9 %copy-start.7 = (bf16[4096,512]{1,0:T(8,128)(2,1)S(1)}, bf16[4096,512]{1,0:T(8,128)(2,1)}, u32[]{:S(2)}) copy-start(bf16[4096,512]{1,0:T(8,128)(2,1)} %all-gather.14.cloned.1.call-done) | copy-start | bytes 12582916
  320.6 1.9 copy-start.9
  328.5 25.9 %copy-start.8 = (bf16[640,2048]{1,0:T(8,128)(2,1)S(1)}, bf16[640,2048]{1,0:T(8,128)(2,1)}, u32[]{:S(2)}) copy-start(bf16[640,2048]{1,0:T(8,128)(2,1)} %convolution_convert_fusion.refs_0_) | copy-start | bytes 7864324
  357.8 36.5 %copy-start.10 = (bf16[512,2048]{1,0:T(8,128)(2,1)S(1)}, bf16[512,2048]{1,0:T(8,128)(2,1)}, u32[]{:S(2)}) copy-start(bf16[512,2048]{1,0:T(8,128)(2,1)} %convolution_convert_fusion.2.refs_0_) | copy-start | bytes 6291460
  368.9 28.9 %copy-start = (bf16[4096,256]{1,0:T(8,128)(2,1)S(1)}, bf16[4096,256]{1,0:T(8,128)(2,1)}, u32[]{:S(2)}) copy-start(bf16[4096,256]{1,0:T(8,128)(2,1)} %all-gather.12.cloned.1.call-done) | copy-start | bytes 6291460
  368.9 28.9 %copy-start.1 = (bf16[256,2048]{1,0:T(8,128)(2,1)S(1)}, bf16[256,2048]{1,0:T(8,128)(2,1)}, u32[]{:S(2)}) copy-start(bf16[256,2048]{1,0:T(8,128)(2,1)} %place.6.weight_ref) | copy-start | bytes 3145732
  403.3 19.6 %collective-permute-start.7 = (bf16[1024,2048]{1,0:T(8,128)(2,1)}, bf16[1024,2048]{1,0:T(8,128)(2,1)}, u32[]{:S(2)}, u32[]{:S(2)}) collective-permute-start(bf16[1024,2048]{1,0:T(8,128)(2,1)} %project.13.refs_0_), channel_id=1, source_target_pairs={{0,1},{1,0},{2,3},{3,2},{4,5},{5,4},{6,7},{7,6},{8,9},{9,8},{10,11... | collective-permute-start | bytes 12582920 | tf_op jit(solution)/shard_map/ppermute | solution.py:173
  408.9 20.1 %collective-permute-start.6 = (bf16[1024,2048]{1,0:T(8,128)(2,1)}, bf16[1024,2048]{1,0:T(8,128)(2,1)}, u32[]{:S(2)}, u32[]{:S(2)}) collective-permute-start(bf16[1024,2048]{1,0:T(8,128)(2,1)} %project.12.refs_0_), channel_id=1, source_target_pairs={{0,1},{1,0},{2,3},{3,2},{4,5},{5,4},{6,7},{7,6},{8,9},{9,8},{10,11... | collective-permute-start | bytes 12582920 | tf_op jit(solution)/shard_map/ppermute | solution.py:173
  414.9 7.5 %copy-start.12 = (s32[1,1,256]{2,1,0:T(1,128)S(1)}, s32[1,1,256]{2,1,0:T(1,128)}, u32[]{:S(2)}) copy-start(s32[1,1,256]{2,1,0:T(1,128)} %param.7) | copy-start | bytes 3076
  414.9 20.1 %collective-permute-start.5 = (bf16[1024,2048]{1,0:T(8,128)(2,1)}, bf16[1024,2048]{1,0:T(8,128)(2,1)}, u32[]{:S(2)}, u32[]{:S(2)}) collective-permute-start(bf16[1024,2048]{1,0:T(8,128)(2,1)} %project.11.refs_0_), channel_id=1, source_target_pairs={{0,1},{1,0},{2,3},{3,2},{4,5},{5,4},{6,7},{7,6},{8,9},{9,8},{10,11... | collective-permute-start | bytes 12582920 | tf_op jit(solution)/shard_map/ppermute | solution.py:173
  420.4 39.9 %collective-permute-start.4 = (bf16[1024,2048]{1,0:T(8,128)(2,1)}, bf16[1024,2048]{1,0:T(8,128)(2,1)}, u32[]{:S(2)}, u32[]{:S(2)}) collective-permute-start(bf16[1024,2048]{1,0:T(8,128)(2,1)} %project.10.refs_0_), channel_id=1, source_target_pairs={{0,1},{1,0},{2,3},{3,2},{4,5},{5,4},{6,7},{7,6},{8,9},{9,8},{10,11... | collective-permute-start | bytes 12582920 | tf_op jit(solution)/shard_map/ppermute | solution.py:173
  420.9 25.1 %collective-permute-start.8 = (bf16[256,2048]{1,0:T(8,128)(2,1)S(1)}, bf16[256,2048]{1,0:T(8,128)(2,1)S(1)}, u32[]{:S(2)}, u32[]{:S(2)}) collective-permute-start(bf16[256,2048]{1,0:T(8,128)(2,1)S(1)} %convolution_convert_fusion.3.refs_0_), channel_id=1, source_target_pairs={{0,2},{2,0},{1,3},{3,1},{4,6},{6,4},{5,7},{7,5},{8,10},{10,8},{9,1... | collective-permute-start | bytes 3145736 | tf_op jit(solution)/shard_map/ppermute | solution.py:173
Sparse Core Ops, SparseCore 0:
  10.8 100.7 all-gather.7
  113.2 96.4 all-gather.9
  211.2 79.1 all-gather.13
  291.8 44.4 all-gather.11
